TPU v7x, 128 devices: a whole 4x4x4 slice. The times are simulated.
128 devices in a mesh: section: 2 (over core), row: 4 (over y), col: 16 (over x, z).
Axes of the slice: x: 4, y: 4, z: 4, core: 2. Of those that a mesh axis runs over, the one named last changes fastest.
Arguments:
- block_input: bfloat16 [2, 4096, 1024], P(None, 'col', 'row'), may hold values from -30 to 30
- cotangent: bfloat16 [2, 4096, 1024], P(None, 'col', 'row'), may hold values from -6 to 6
- images_used: int32 [2], replicated, may hold values from 1 to 4, as said below
- norm1_gain: float32 [2, 1024], P('section', 'row'), may hold values from 0.5 to 1.5
- norm1_bias: float32 [2, 1024], P('section', 'row'), may hold values from -1.75 to 1.75
- qkv_weight: bfloat16 [2, 1024, 3072], P('section', 'row', 'col'), may hold values from -0.1875 to 0.1875
- query_bias: float32 [2, 1024], P('section', 'col'), may hold values from -1.75 to 1.75
- value_bias: float32 [2, 1024], P('section', 'col'), may hold values from -0.625 to 0.625
- proj_weight: bfloat16 [2, 1024, 1024], P('section', 'col', 'row'), may hold values from -1.5 to 1.5
- proj_bias: float32 [2, 1024], P('section', 'row'), may hold values from -1.75 to 1.75
- attn_scale: float32 [2, 1024], P('section', 'row'), may hold values from 0.5 to 1.5
- norm2_gain: float32 [2, 1024], P('section', 'row'), may hold values from 0.5 to 1.5
- norm2_bias: float32 [2, 1024], P('section', 'row'), may hold values from -1.75 to 1.75
- inner_weight: bfloat16 [2, 1024, 4096], P('section', 'row', 'col'), may hold values from -0.1875 to 0.1875
- inner_bias: float32 [2, 4096], P('section', 'col'), may hold values from -1.75 to 1.75
- outer_weight: bfloat16 [2, 4096, 1024], P('section', 'col', 'row'), may hold values from -0.09375 to 0.09375
- outer_bias: float32 [2, 1024], P('section', 'row'), may hold values from -1.75 to 1.75
- mlp_scale: float32 [2, 1024], P('section', 'row'), may hold values from 0.5 to 1.5
Outputs:
- boundary: float32 [2, 2, 4096, 1024], P('section', None, 'col', 'row')
- grad_norm1_gain: float32 [2, 1024], P('section', 'row')
- grad_norm1_bias: float32 [2, 1024], P('section', 'row')
- grad_qkv_weight: float32 [2, 1024, 3072], P('section', 'row', 'col')
- grad_query_bias: float32 [2, 1024], P('section', 'col')
- grad_value_bias: float32 [2, 1024], P('section', 'col')
- grad_proj_weight: float32 [2, 1024, 1024], P('section', 'col', 'row')
- grad_proj_bias: float32 [2, 1024], P('section', 'row')
- grad_attn_scale: float32 [2, 1024], P('section', 'row')
- grad_norm2_gain: float32 [2, 1024], P('section', 'row')
- grad_norm2_bias: float32 [2, 1024], P('section', 'row')
- grad_inner_weight: float32 [2, 1024, 4096], P('section', 'row', 'col')
- grad_inner_bias: float32 [2, 4096], P('section', 'col')
- grad_outer_weight: float32 [2, 4096, 1024], P('section', 'col', 'row')
- grad_outer_bias: float32 [2, 1024], P('section', 'row')
- grad_mlp_scale: float32 [2, 1024], P('section', 'row')
Inputs may be any that keep to these rules, and one draw needn't show every extreme that they name: Micro-batch m holds images in its first images_used[m] slots of 1024 tokens; its other slots are empty. Some micro-batch is full in every draw.
All inputs are finite; a program needn't handle non-finite values.
Results may differ from a plain program's by a relative error of at most 0.02.
Values may be sent and summed in bfloat16 or wider, within the bound.
No kernel may reach another device: no remote copies, remote signals or barrier semaphores. Data moves between devices by JAX's collectives and lax.ppermute only.
A program may use at most 192 MiB of HBM per device.

v0:
```python
import jax
import jax.numpy as jnp
from jax import lax
from jax.sharding import PartitionSpec as P

HD = 64
LENGTH = 1024


norm_eps = 1e-06


def from_everyone(shard, axis):
    copies = jnp.broadcast_to(shard, (lax.axis_size(axis), *shard.shape))
    return lax.all_to_all(copies, axis, split_axis=0, concat_axis=0, tiled=True)


def in_order(tiles, dim):
    tiles = jnp.moveaxis(tiles, 0, dim)
    lengths = tiles.shape
    return tiles.reshape(*lengths[:dim], lengths[dim] * lengths[dim + 1], *lengths[dim + 2 :])


def collect(shard, axis, dim):
    tiles = from_everyone(shard, axis)
    return in_order(tiles, dim)


def cut_along(shard, dim, count):
    before, after = (shard.shape[:dim], shard.shape[dim + 1 :])
    return jnp.moveaxis(shard.reshape(*before, count, -1, *after), dim, 0)


def sum_at_owner(shard, axis, dim):
    tiles = cut_along(shard, dim, lax.axis_size(axis))
    arrived = lax.all_to_all(tiles, axis, split_axis=0, concat_axis=0, tiled=True)
    return arrived.astype(jnp.float32).sum(axis=0)


def shifted(shard, axis, by):
    count = lax.axis_size(axis)
    pairs = [(i, i + by) for i in range(count) if 0 <= i + by < count]
    return lax.ppermute(shard, axis, pairs)


def taken_together(shard, axis):
    return from_everyone(shard, axis).sum(axis=0)


def together(arrays, axis):
    ravelled, at, finished = (jnp.concatenate([a.reshape(-1) for a in arrays]), 0, [])
    total = taken_together(ravelled, axis)
    for a in arrays:
        finished.append(total[at : at + a.size].reshape(a.shape))
        at += a.size
    return tuple(finished)


def gather_cols(sharded):
    return collect(sharded, "col", 0)


def product_term(gathered, matrix, flipped):
    if flipped:
        return lax.dot_general(
            gathered, matrix, (((1,), (1,)), ((), ())), preferred_element_type=jnp.float32
        )
    return jnp.dot(gathered, matrix, preferred_element_type=jnp.float32)


def sum_cols(gathered, matrix, flipped):
    return sum_at_owner(product_term(gathered, matrix, flipped).astype(jnp.bfloat16), "col", 0)


def weight_grad(gathered_in, gathered_out):
    return lax.dot_general(
        gathered_in, gathered_out, (((0,), (0,)), ((), ())), preferred_element_type=jnp.float32
    )


def flipped_product(left_rows, matrix):
    return lax.dot_general(
        left_rows, matrix, (((1,), (1,)), ((), ())), preferred_element_type=jnp.float32
    )


def exact_gelu(pre_act):
    return jax.nn.gelu(pre_act, approximate=False)


def norm_local(features, norm_gain, norm_shift):
    center = jnp.mean(features, axis=-1, keepdims=True)
    offset = features - center
    spread = jnp.mean(offset * offset, axis=-1, keepdims=True)
    inverse = lax.rsqrt(spread + norm_eps)
    scaled = offset * inverse
    return (scaled * norm_gain + norm_shift, scaled, inverse[:, 0])


def norm_back_local(upstream, scaled, inverse, norm_gain):
    weighted = upstream * norm_gain
    first_mean = jnp.mean(weighted, axis=-1, keepdims=True)
    second_mean = jnp.mean(weighted * scaled, axis=-1, keepdims=True)
    result = inverse[:, None] * (weighted - first_mean - scaled * second_mean)
    return (result, jnp.sum(upstream * scaled, axis=0), jnp.sum(upstream, axis=0))


def head_items(triples):
    images = triples.shape[0] // LENGTH
    heads_here = triples.shape[1] // (3 * HD)
    shaped = triples.reshape(images, LENGTH, heads_here, 3, HD)
    return jnp.transpose(shaped, (0, 2, 3, 1, 4)).reshape(images * heads_here, 3, LENGTH, HD)


def attend_item(head_item):
    scores = jnp.einsum(
        "qd,kd->qk", head_item[0], head_item[1], preferred_element_type=jnp.float32
    ) * HD ** (-0.5)
    row_peak = jnp.max(scores, axis=-1, keepdims=True)
    raised = jnp.exp(scores - row_peak)
    row_total = jnp.sum(raised, axis=-1, keepdims=True)
    weights_low = (raised / row_total).astype(jnp.bfloat16)
    mixed_rows = jnp.einsum(
        "qk,kd->qd", weights_low, head_item[2], preferred_element_type=jnp.float32
    )
    return (mixed_rows.astype(jnp.bfloat16), (row_peak + jnp.log(row_total))[:, 0])


def attention_forward(triples):
    images = triples.shape[0] // LENGTH
    heads_here = triples.shape[1] // (3 * HD)
    mixed_items, log_totals = lax.map(attend_item, head_items(triples))
    merged = jnp.transpose(mixed_items.reshape(images, heads_here, LENGTH, HD), (0, 2, 1, 3))
    return (merged.reshape(triples.shape[0], heads_here * HD), log_totals)


def attend_back(packed):
    head_item, upstream, log_total = packed
    scores = jnp.einsum(
        "qd,kd->qk", head_item[0], head_item[1], preferred_element_type=jnp.float32
    ) * HD ** (-0.5)
    attn_probs = jnp.exp(scores - log_total[:, None])
    grad_values = jnp.einsum(
        "qk,qd->kd", attn_probs.astype(jnp.bfloat16), upstream, preferred_element_type=jnp.float32
    )
    grad_probs = jnp.einsum("qd,kd->qk", upstream, head_item[2], preferred_element_type=jnp.float32)
    along_row = jnp.sum(attn_probs * grad_probs, axis=-1, keepdims=True)
    grad_scores = (attn_probs * (grad_probs - along_row)).astype(jnp.bfloat16)
    grad_queries = jnp.einsum(
        "qk,kd->qd", grad_scores, head_item[1], preferred_element_type=jnp.float32
    ) * HD ** (-0.5)
    grad_keys = jnp.einsum(
        "qk,qd->kd", grad_scores, head_item[0], preferred_element_type=jnp.float32
    ) * HD ** (-0.5)
    return jnp.stack([grad_queries, grad_keys, grad_values], axis=0)


def attention_backward(triples, grad_mixed, log_totals):
    images = triples.shape[0] // LENGTH
    heads_here = triples.shape[1] // (3 * HD)
    upstream = jnp.transpose(grad_mixed.reshape(images, LENGTH, heads_here, HD), (0, 2, 1, 3))
    upstream = upstream.reshape(images * heads_here, LENGTH, HD)
    grad_items = lax.map(attend_back, (head_items(triples), upstream, log_totals))
    shaped = jnp.transpose(grad_items.reshape(images, heads_here, 3, LENGTH, HD), (0, 3, 1, 2, 4))
    return shaped.reshape(triples.shape[0], heads_here * 3 * HD)


def build_joint_bias(query_bias, value_bias):
    heads_here = query_bias.shape[0] // HD
    return jnp.stack(
        [
            query_bias.reshape(heads_here, HD),
            jnp.zeros((heads_here, HD), jnp.float32),
            value_bias.reshape(heads_here, HD),
        ],
        axis=1,
    ).reshape(-1)


def token_order(rows):
    col_count = lax.axis_size("col")
    per_group = col_count // lax.axis_size("row")
    piece = rows.shape[0] // (col_count * per_group)
    shaped = rows.reshape(col_count, per_group, piece, rows.shape[1])
    return jnp.transpose(shaped, (1, 0, 2, 3)).reshape(rows.shape)


def device_order(rows):
    col_count = lax.axis_size("col")
    per_group = col_count // lax.axis_size("row")
    piece = rows.shape[0] // (col_count * per_group)
    shaped = rows.reshape(per_group, col_count, piece, rows.shape[1])
    return jnp.transpose(shaped, (1, 0, 2, 3)).reshape(rows.shape)


def forward_wide(features, weights):
    (
        gain_one,
        shift_one,
        joint_weight,
        query_bias,
        value_bias,
        proj_weight,
        proj_bias,
        scale_one,
        gain_two,
        shift_two,
        inner_weight,
        inner_bias,
        outer_weight,
        outer_bias,
        scale_two,
    ) = weights
    first_norm, first_scaled, first_inverse = norm_local(features, gain_one, shift_one)
    first_gathered = gather_cols(first_norm.astype(jnp.bfloat16))
    joint_bias = build_joint_bias(query_bias, value_bias)
    joint_rows = (
        jnp.dot(first_gathered, joint_weight, preferred_element_type=jnp.float32) + joint_bias
    )
    triples = token_order(joint_rows.astype(jnp.bfloat16))
    mixed_heads, log_totals = attention_forward(triples)
    heads_local = device_order(mixed_heads)
    attended = sum_cols(heads_local, proj_weight, False) + proj_bias
    hidden = features + scale_one * attended
    second_norm, second_scaled, second_inverse = norm_local(hidden, gain_two, shift_two)
    second_gathered = gather_cols(second_norm.astype(jnp.bfloat16))
    expanded = (
        jnp.dot(second_gathered, inner_weight, preferred_element_type=jnp.float32) + inner_bias
    )
    active_local = exact_gelu(expanded).astype(jnp.bfloat16)
    contracted = sum_cols(active_local, outer_weight, False) + outer_bias
    layer_out = hidden + scale_two * contracted
    saved_values = (
        first_scaled,
        first_inverse,
        first_gathered,
        triples,
        heads_local,
        log_totals,
        attended,
        second_scaled,
        second_inverse,
        second_gathered,
        expanded,
        active_local,
        contracted,
    )
    return (layer_out, saved_values)


def backward_wide(saved_values, grad_output, weights):
    (
        gain_one,
        shift_one,
        joint_weight,
        query_bias,
        value_bias,
        proj_weight,
        proj_bias,
        scale_one,
        gain_two,
        shift_two,
        inner_weight,
        inner_bias,
        outer_weight,
        outer_bias,
        scale_two,
    ) = weights
    (
        first_scaled,
        first_inverse,
        first_gathered,
        triples,
        heads_local,
        log_totals,
        attended,
        second_scaled,
        second_inverse,
        second_gathered,
        expanded,
        active_local,
        contracted,
    ) = saved_values
    grad_scale_two = jnp.sum(grad_output * contracted, axis=0)
    outer_gathered = gather_cols((grad_output * scale_two).astype(jnp.bfloat16))
    grad_outer_weight = weight_grad(active_local, outer_gathered)
    grad_outer_bias = jnp.sum(outer_gathered.astype(jnp.float32), axis=0)
    grad_active = flipped_product(outer_gathered, outer_weight)
    tangent = jax.vjp(exact_gelu, expanded)[1](grad_active)[0]
    grad_expanded = tangent.astype(jnp.bfloat16)
    grad_inner_weight = weight_grad(second_gathered, grad_expanded)
    grad_inner_bias = jnp.sum(grad_expanded.astype(jnp.float32), axis=0)
    grad_second = sum_cols(grad_expanded, inner_weight, True)
    grad_hidden_norm, grad_gain_two, grad_shift_two = norm_back_local(
        grad_second, second_scaled, second_inverse, gain_two
    )
    grad_hidden = grad_output + grad_hidden_norm
    grad_scale_one = jnp.sum(grad_hidden * attended, axis=0)
    attend_gathered = gather_cols((grad_hidden * scale_one).astype(jnp.bfloat16))
    grad_proj_weight = weight_grad(heads_local, attend_gathered)
    grad_proj_bias = jnp.sum(attend_gathered.astype(jnp.float32), axis=0)
    grad_heads = flipped_product(attend_gathered, proj_weight).astype(jnp.bfloat16)
    grad_tokens = attention_backward(triples, token_order(grad_heads), log_totals).astype(
        jnp.bfloat16
    )
    grad_triples = device_order(grad_tokens)
    grad_joint_weight = weight_grad(first_gathered, grad_triples)
    heads_here = query_bias.shape[0] // HD
    column_sums = jnp.sum(grad_triples.astype(jnp.float32), axis=0).reshape(heads_here, 3, HD)
    grad_query_bias = column_sums[:, 0, :].reshape(-1)
    grad_value_bias = column_sums[:, 2, :].reshape(-1)
    grad_first = sum_cols(grad_triples, joint_weight, True)
    grad_input_norm, grad_gain_one, grad_shift_one = norm_back_local(
        grad_first, first_scaled, first_inverse, gain_one
    )
    grad_input = grad_hidden + grad_input_norm
    layer_grads = (
        grad_gain_one,
        grad_shift_one,
        grad_joint_weight,
        grad_query_bias,
        grad_value_bias,
        grad_proj_weight,
        grad_proj_bias,
        grad_scale_one,
        grad_gain_two,
        grad_shift_two,
        grad_inner_weight,
        grad_inner_bias,
        grad_outer_weight,
        grad_outer_bias,
        grad_scale_two,
    )
    return (grad_input, layer_grads)


def run_sections(layer_rows, cot_rows, images_used, weights, slot_index, forward_fn, backward_fn):
    is_first = lax.axis_index("section") == 0
    batches = layer_rows.shape[0]
    empty_rows = jnp.zeros(layer_rows.shape[1:], jnp.float32)
    arrived = empty_rows
    section_inputs = []
    stash_list = []
    finals = []
    for step_fwd in range(batches + 1):
        if step_fwd < batches:
            fresh_rows = layer_rows[step_fwd].astype(jnp.float32)
        else:
            fresh_rows = empty_rows
        layer_in = jnp.where(is_first, fresh_rows, arrived)
        section_inputs.append(layer_in)
        layer_out, saved_values = forward_fn(layer_in, weights)
        stash_list.append(saved_values)
        if step_fwd >= 1:
            live_mask = (slot_index < images_used[step_fwd - 1]).astype(jnp.float32)[:, None]
            finals.append(layer_out * live_mask)
        if step_fwd < batches:
            arrived = shifted(layer_out.astype(jnp.bfloat16), "section", 1).astype(jnp.float32)
    returned = empty_rows
    totals = None
    input_grads = [empty_rows] * batches
    for step_back in range(batches + 1):
        if step_back < batches:
            batch_index = batches - 1 - step_back
            live_mask = (slot_index < images_used[batch_index]).astype(jnp.float32)[:, None]
            seeded = cot_rows[batch_index].astype(jnp.float32) * live_mask
        else:
            seeded = empty_rows
        upstream = jnp.where(is_first, returned, seeded)
        position = batches - step_back
        saved_values = stash_list[position]
        grad_input, layer_grads = backward_fn(saved_values, upstream, weights)
        if totals is None:
            totals = layer_grads
        else:
            totals = jax.tree.map(jnp.add, totals, layer_grads)
        if step_back >= 1:
            input_grads[batches - step_back] = grad_input
        if step_back < batches:
            returned = shifted(grad_input.astype(jnp.bfloat16), "section", -1).astype(jnp.float32)
    edge_values = jnp.where(is_first, jnp.stack(input_grads, axis=0), jnp.stack(finals, axis=0))
    return (edge_values, totals)


def local(
    block_input,
    cotangent,
    images_used,
    norm1_gain,
    norm1_bias,
    qkv_weight,
    query_bias,
    value_bias,
    proj_weight,
    proj_bias,
    attn_scale,
    norm2_gain,
    norm2_bias,
    inner_weight,
    inner_bias,
    outer_weight,
    outer_bias,
    mlp_scale,
):
    weights = tuple(
        (
            stacked[0]
            for stacked in (
                norm1_gain,
                norm1_bias,
                qkv_weight,
                query_bias,
                value_bias,
                proj_weight,
                proj_bias,
                attn_scale,
                norm2_gain,
                norm2_bias,
                inner_weight,
                inner_bias,
                outer_weight,
                outer_bias,
                mlp_scale,
            )
        )
    )
    block_rows = block_input.shape[1]
    wide_mats = (
        lax.all_gather(weights[2], "row", axis=0, tiled=True),
        lax.all_gather(weights[5], "row", axis=1, tiled=True),
        lax.all_gather(weights[10], "row", axis=0, tiled=True),
        lax.all_gather(weights[12], "row", axis=1, tiled=True),
    )
    wide_vecs = (
        lax.all_gather(weights[0], "row", axis=0, tiled=True),
        lax.all_gather(weights[1], "row", axis=0, tiled=True),
        lax.all_gather(weights[6], "row", axis=0, tiled=True),
        lax.all_gather(weights[7], "row", axis=0, tiled=True),
        lax.all_gather(weights[8], "row", axis=0, tiled=True),
        lax.all_gather(weights[9], "row", axis=0, tiled=True),
        lax.all_gather(weights[13], "row", axis=0, tiled=True),
        lax.all_gather(weights[14], "row", axis=0, tiled=True),
    )
    wide_weights = (
        wide_vecs[0],
        wide_vecs[1],
        wide_mats[0],
        weights[3],
        weights[4],
        wide_mats[1],
        wide_vecs[2],
        wide_vecs[3],
        wide_vecs[4],
        wide_vecs[5],
        wide_mats[2],
        weights[11],
        wide_mats[3],
        wide_vecs[6],
        wide_vecs[7],
    )
    paired = jnp.stack([block_input, cotangent], axis=0)
    spread_cols = lax.all_to_all(paired, "col", split_axis=2, concat_axis=2, tiled=True)
    entered = lax.all_to_all(spread_cols, "row", split_axis=2, concat_axis=3, tiled=True)
    col_count = lax.axis_size("col")
    row_count = lax.axis_size("row")
    per_group = col_count // row_count
    piece = block_rows // col_count
    group_ids = lax.axis_index("row") * per_group + jnp.arange(per_group, dtype=jnp.int32)
    token_index = (
        group_ids[:, None] * block_rows
        + lax.axis_index("col") * piece
        + jnp.arange(piece, dtype=jnp.int32)[None, :]
    ).reshape(-1)
    slot_index = token_index // LENGTH
    edge_rows, wide_totals = run_sections(
        entered[0], entered[1], images_used, wide_weights, slot_index, forward_wide, backward_wide
    )
    edge_values = lax.all_to_all(
        lax.all_to_all(
            edge_rows.astype(jnp.bfloat16), "row", split_axis=2, concat_axis=1, tiled=True
        ),
        "col",
        split_axis=1,
        concat_axis=1,
        tiled=True,
    ).astype(edge_rows.dtype)

    def tiled(vector):
        return jnp.broadcast_to(vector[None, :], (row_count, vector.shape[0]))

    parts = (
        lax.psum_scatter(
            wide_totals[2].astype(jnp.bfloat16), "row", scatter_dimension=0, tiled=True
        ).astype(jnp.float32),
        lax.psum_scatter(
            wide_totals[5].astype(jnp.bfloat16), "row", scatter_dimension=1, tiled=True
        ).astype(jnp.float32),
        lax.psum_scatter(
            wide_totals[10].astype(jnp.bfloat16), "row", scatter_dimension=0, tiled=True
        ).astype(jnp.float32),
        lax.psum_scatter(
            wide_totals[12].astype(jnp.bfloat16), "row", scatter_dimension=1, tiled=True
        ).astype(jnp.float32),
        lax.psum_scatter(
            wide_totals[0].astype(jnp.bfloat16), "row", scatter_dimension=0, tiled=True
        ).astype(jnp.float32),
        lax.psum_scatter(
            wide_totals[1].astype(jnp.bfloat16), "row", scatter_dimension=0, tiled=True
        ).astype(jnp.float32),
        lax.psum_scatter(
            wide_totals[6].astype(jnp.bfloat16), "row", scatter_dimension=0, tiled=True
        ).astype(jnp.float32),
        lax.psum_scatter(
            wide_totals[7].astype(jnp.bfloat16), "row", scatter_dimension=0, tiled=True
        ).astype(jnp.float32),
        lax.psum_scatter(
            wide_totals[8].astype(jnp.bfloat16), "row", scatter_dimension=0, tiled=True
        ).astype(jnp.float32),
        lax.psum_scatter(
            wide_totals[9].astype(jnp.bfloat16), "row", scatter_dimension=0, tiled=True
        ).astype(jnp.float32),
        lax.psum_scatter(
            wide_totals[13].astype(jnp.bfloat16), "row", scatter_dimension=0, tiled=True
        ).astype(jnp.float32),
        lax.psum_scatter(
            wide_totals[14].astype(jnp.bfloat16), "row", scatter_dimension=0, tiled=True
        ).astype(jnp.float32),
        lax.psum_scatter(
            tiled(wide_totals[3]).astype(jnp.bfloat16), "row", scatter_dimension=0, tiled=True
        ).astype(jnp.float32),
        lax.psum_scatter(
            tiled(wide_totals[4]).astype(jnp.bfloat16), "row", scatter_dimension=0, tiled=True
        ).astype(jnp.float32),
        lax.psum_scatter(
            tiled(wide_totals[11]).astype(jnp.bfloat16), "row", scatter_dimension=0, tiled=True
        ).astype(jnp.float32),
    )
    totals = (
        parts[4],
        parts[5],
        parts[0],
        parts[12].reshape(-1),
        parts[13].reshape(-1),
        parts[1],
        parts[6],
        parts[7],
        parts[8],
        parts[9],
        parts[2],
        parts[14].reshape(-1),
        parts[3],
        parts[10],
        parts[11],
    )
    summed = together((totals[0], totals[1], totals[7], totals[8], totals[9], totals[14]), "col")
    return (
        edge_values[None],
        summed[0][None],
        summed[1][None],
        totals[2][None],
        totals[3][None],
        totals[4][None],
        totals[5][None],
        totals[6][None],
        summed[2][None],
        summed[3][None],
        summed[4][None],
        totals[10][None],
        totals[11][None],
        totals[12][None],
        totals[13][None],
        summed[5][None],
    )


def solution(mesh):
    placed = (
        P(None, "col", "row"),
        P(None, "col", "row"),
        P(),
        P("section", "row"),
        P("section", "row"),
        P("section", "row", "col"),
        P("section", "col"),
        P("section", "col"),
        P("section", "col", "row"),
        P("section", "row"),
        P("section", "row"),
        P("section", "row"),
        P("section", "row"),
        P("section", "row", "col"),
        P("section", "col"),
        P("section", "col", "row"),
        P("section", "row"),
        P("section", "row"),
    )
    return jax.shard_map(
        local,
        mesh=mesh,
        in_specs=placed,
        out_specs=(
            P("section", None, "col", "row"),
            P("section", "row"),
            P("section", "row"),
            P("section", "row", "col"),
            P("section", "col"),
            P("section", "col"),
            P("section", "col", "row"),
            P("section", "row"),
            P("section", "row"),
            P("section", "row"),
            P("section", "row"),
            P("section", "row", "col"),
            P("section", "col"),
            P("section", "col", "row"),
            P("section", "row"),
            P("section", "row"),
        ),
        check_vma=False,
    )
```

profile of v0, /device:TPU:1, one launch (start us, length us, event | category | flops | bytes accessed | tf_op | source)
XLA Modules:
  0.0 1053.5 jit_solution(7106940132150507894)
XLA Ops:
  9.5 18.6 %all_to_all.169 = bf16[2,2,256,256]{3,1,0,2:T(2,128)(2,1)} all-to-all(bf16[2,2,256,256]{3,1,0,2:T(2,128)(2,1)S(1)} %pad_maximum_fusion), channel_id=1, replica_groups=mesh['section'=2,'row'=4,'col'=16] {'col'}, dimensions={2} | all-to-all | bytes 1048576 | tf_op jit(solution)/shard_map/all_to_all | solution.py:462
  32.3 8.9 all-gather.1
  53.8 9.1 all-gather.4
  62.9 10.7 %all-gather.3 = bf16[1,1024,192]{1,2,0:T(8,128)(2,1)S(1)} all-gather(bf16[1,256,192]{1,2,0:T(8,128)(2,1)S(1)} %copy-done.115), channel_id=5, replica_groups=mesh['section'=2,'row'=4,'col'=16] {'row'}, dimensions={1}, use_global_device_ids=true | all-gather | bytes 491520 | tf_op jit(solution)/shard_map/all_gather | solution.py:429
  91.5 8.2 all-to-all-start.3
  137.2 9.9 all-gather.9
  147.1 11.2 %all-gather.10 = bf16[1,256,1024]{2,1,0:T(8,128)(2,1)S(1)} all-gather(bf16[1,256,256]{2,1,0:T(8,128)(2,1)S(1)} %copy-done.114), channel_id=12, replica_groups=mesh['section'=2,'row'=4,'col'=16] {'row'}, dimensions={2}, use_global_device_ids=true | all-gather | bytes 655360 | tf_op jit(solution)/shard_map/all_gather | solution.py:432
  173.2 7.4 all-gather.11
  194.6 20.1 %collective-permute-done = bf16[64,1024]{1,0:T(8,128)(2,1)S(1)} collective-permute-done((bf16[64,1024]{1,0:T(8,128)(2,1)S(1)}, bf16[64,1024]{1,0:T(8,128)(2,1)S(1)}, u32[]{:S(2)}, u32[]{:S(2)}) %collective-permute-start) | collective-permute-done | bytes 131104 | tf_op jit(solution)/shard_map/ppermute | solution.py:43
  215.6 31.5 %all_to_all.170 = bf16[16,64,1024]{2,1,0:T(8,128)(2,1)S(1)} all-to-all(bf16[16,64,1024]{2,1,0:T(8,128)(2,1)S(1)} %broadcast_in_dim.132), channel_id=1, replica_groups=mesh['section'=2,'row'=4,'col'=16] {'col'}, dimensions={0} | all-to-all | bytes 4194304 | tf_op jit(solution)/shard_map/all_to_all | solution.py:15
  258.9 29.5 %all_to_all.171 = bf16[16,64,1024]{2,1,0:T(8,128)(2,1)S(1)} all-to-all(bf16[16,64,1024]{2,1,0:T(8,128)(2,1)S(1)} %bitcast.403), channel_id=1, replica_groups=mesh['section'=2,'row'=4,'col'=16] {'col'}, dimensions={0} | all-to-all | bytes 4194304 | tf_op jit(solution)/shard_map/all_to_all | solution.py:36
  290.7 28.6 %all_to_all.172 = bf16[16,64,1024]{2,1,0:T(8,128)(2,1)S(1)} all-to-all(bf16[16,64,1024]{2,1,0:T(8,128)(2,1)S(1)} %broadcast_in_dim.133), channel_id=1, replica_groups=mesh['section'=2,'row'=4,'col'=16] {'col'}, dimensions={0} | all-to-all | bytes 4194304 | tf_op jit(solution)/shard_map/all_to_all | solution.py:15
  333.3 21.0 %all-to-all-done.9 = bf16[16,64,1024]{2,1,0:T(8,128)(2,1)S(1)} async-done(((bf16[16,64,1024]{2,1,0:T(8,128)(2,1)}), bf16[16,64,1024]{2,1,0:T(8,128)(2,1)S(1)}, u32[]{:S(2)}, u32[]{:S(2)}) %all-to-all-start.9) | async-done | bytes 2097184 | tf_op jit(solution)/shard_map/all_to_all | solution.py:36
  365.9 30.8 %all_to_all.173 = bf16[16,64,1024]{2,1,0:T(8,128)(2,1)S(1)} all-to-all(bf16[16,64,1024]{2,1,0:T(8,128)(2,1)S(1)} %broadcast_in_dim.134), channel_id=1, replica_groups=mesh['section'=2,'row'=4,'col'=16] {'col'}, dimensions={0} | all-to-all | bytes 4194304 | tf_op jit(solution)/shard_map/all_to_all | solution.py:15
  409.2 29.7 %all_to_all.174 = bf16[16,64,1024]{2,1,0:T(8,128)(2,1)S(1)} all-to-all(bf16[16,64,1024]{2,1,0:T(8,128)(2,1)S(1)} %bitcast.404), channel_id=1, replica_groups=mesh['section'=2,'row'=4,'col'=16] {'col'}, dimensions={0} | all-to-all | bytes 4194304 | tf_op jit(solution)/shard_map/all_to_all | solution.py:36
  440.3 30.8 %all_to_all.175 = bf16[16,64,1024]{2,1,0:T(8,128)(2,1)} all-to-all(bf16[16,64,1024]{2,1,0:T(8,128)(2,1)S(1)} %broadcast_in_dim.240), channel_id=1, replica_groups=mesh['section'=2,'row'=4,'col'=16] {'col'}, dimensions={0} | all-to-all | bytes 4194304 | tf_op jit(solution)/shard_map/all_to_all | solution.py:15
  482.6 19.2 %all-to-all-done.13 = bf16[16,64,1024]{2,1,0:T(8,128)(2,1)S(1)} async-done(((bf16[16,64,1024]{2,1,0:T(8,128)(2,1)}), bf16[16,64,1024]{2,1,0:T(8,128)(2,1)S(1)}, u32[]{:S(2)}, u32[]{:S(2)}) %all-to-all-start.13) | async-done | bytes 2097184 | tf_op jit(solution)/shard_map/all_to_all | solution.py:15
  506.6 30.9 %all_to_all.176 = bf16[16,64,1024]{2,1,0:T(8,128)(2,1)S(1)} all-to-all(bf16[16,64,1024]{2,1,0:T(8,128)(2,1)S(1)} %bitcast.405), channel_id=1, replica_groups=mesh['section'=2,'row'=4,'col'=16] {'col'}, dimensions={0} | all-to-all | bytes 4194304 | tf_op jit(solution)/shard_map/all_to_all | solution.py:36
  547.5 22.6 %all-to-all-done.15 = bf16[16,64,1024]{2,1,0:T(8,128)(2,1)S(1)} async-done(((bf16[16,64,1024]{2,1,0:T(8,128)(2,1)}), bf16[16,64,1024]{2,1,0:T(8,128)(2,1)S(1)}, u32[]{:S(2)}, u32[]{:S(2)}) %all-to-all-start.15) | async-done | bytes 2097184 | tf_op jit(solution)/shard_map/all_to_all | solution.py:15
  583.7 31.4 %all_to_all.177 = bf16[16,64,1024]{2,1,0:T(8,128)(2,1)S(1)} all-to-all(bf16[16,64,1024]{2,1,0:T(8,128)(2,1)S(1)} %bitcast.406), channel_id=1, replica_groups=mesh['section'=2,'row'=4,'col'=16] {'col'}, dimensions={0} | all-to-all | bytes 4194304 | tf_op jit(solution)/shard_map/all_to_all | solution.py:36
  625.6 30.4 %all_to_all.178 = bf16[16,64,1024]{2,1,0:T(8,128)(2,1)S(1)} all-to-all(bf16[16,64,1024]{2,1,0:T(8,128)(2,1)S(1)} %broadcast_in_dim.243), channel_id=1, replica_groups=mesh['section'=2,'row'=4,'col'=16] {'col'}, dimensions={0} | all-to-all | bytes 4194304 | tf_op jit(solution)/shard_map/all_to_all | solution.py:15
  658.5 29.6 %all_to_all.179 = bf16[16,64,1024]{2,1,0:T(8,128)(2,1)S(1)} all-to-all(bf16[16,64,1024]{2,1,0:T(8,128)(2,1)S(1)} %bitcast.407), channel_id=1, replica_groups=mesh['section'=2,'row'=4,'col'=16] {'col'}, dimensions={0} | all-to-all | bytes 4194304 | tf_op jit(solution)/shard_map/all_to_all | solution.py:36
  698.0 24.0 %all-to-all-done.19 = bf16[16,64,1024]{2,1,0:T(8,128)(2,1)S(1)} async-done(((bf16[16,64,1024]{2,1,0:T(8,128)(2,1)}), bf16[16,64,1024]{2,1,0:T(8,128)(2,1)S(1)}, u32[]{:S(2)}, u32[]{:S(2)}) %all-to-all-start.19) | async-done | bytes 2097184 | tf_op jit(solution)/shard_map/all_to_all | solution.py:15
  764.7 11.7 %all-to-all-done.20 = bf16[16,64,1024]{2,1,0:T(8,128)(2,1)} async-done(((bf16[16,64,1024]{2,1,0:T(8,128)(2,1)}), bf16[16,64,1024]{2,1,0:T(8,128)(2,1)}, u32[]{:S(2)}, u32[]{:S(2)}) %all-to-all-start.20) | async-done | bytes 2097184 | tf_op jit(solution)/shard_map/all_to_all | solution.py:36
  776.3 7.2 all-to-all-start.25
  799.4 9.5 all-to-all-done.25
  872.8 7.9 all-to-all-done.22
  903.3 7.3 reduce-scatter.9.cloned.1.call-done
  914.1 9.7 all-to-all-done.23
  953.3 15.3 %reduce-scatter.7.cloned.1.call-done = bf16[64,256]{1,0:T(8,128)(2,1)} async-done(((bf16[64,1024]{1,0:T(8,128)(2,1)}), bf16[64,256]{1,0:T(8,128)(2,1)}) %reduce-scatter.7.cloned.1.call-update) | async-done | bytes 32784 | tf_op jit(solution)/shard_map/reduce_scatter | solution.py:495
  970.0 21.7 %reduce-scatter.5.cloned.1.call-done = bf16[256,192]{0,1:T(8,128)(2,1)} async-done(((bf16[1024,192]{0,1:T(8,128)(2,1)}), bf16[256,192]{0,1:T(8,128)(2,1)}) %reduce-scatter.5.cloned.1.call-update) | async-done | bytes 98320 | tf_op jit(solution)/shard_map/reduce_scatter | solution.py:492
  996.4 11.6 %all-reduce.11 = (bf16[1024]{0:T(1024)(128)(2,1)S(1)}, bf16[1024]{0:T(1024)(128)(2,1)S(1)}, bf16[1024]{0:T(1024)(128)(2,1)S(1)}, bf16[1024]{0:T(1024)(128)(2,1)S...) all-reduce(bf16[1024]{0:T(1024)(128)(2,1)S(1)} %add_convert_fusion., ...), channel_id=14, replica_groups=mesh['section'=2,'row'=4,'col'=16] {'row'}, use_global_device_ids=true, to_apply=%region_48.49.clone | all-reduce | flops 9728 | bytes 38912
  (757 shorter events, 439.9 us)
Async XLA Ops:
  28.1 19.1 %all-to-all-start.1 = ((bf16[2,2,256,256]{3,1,0,2:T(2,128)(2,1)}), bf16[2,2,256,256]{3,1,0,2:T(2,128)(2,1)S(1)}, u32[]{:S(2)}, u32[]{:S(2)}) async-start(bf16[2,2,256,256]{3,1,0,2:T(2,128)(2,1)} %all_to_all.169), calls=%async_computation.1 | async-start | bytes 1048576 | tf_op jit(solution)/shard_map/all_to_all | solution.py:463
  47.3 146.2 %copy-start.24 = (bf16[2,2,256,256]{3,2,1,0:T(8,128)(2,1)}, bf16[2,2,256,256]{3,2,1,0:T(8,128)(2,1)S(1)}, u32[]{:S(2)}) copy-start(bf16[2,2,256,256]{3,2,1,0:T(8,128)(2,1)S(1)} %copy.215) | copy-start | bytes 1572868
  47.9 80.2 %copy-start.43 = (f32[8,8,4,256]{3,1,2,0:T(8,128)}, f32[8,8,4,256]{3,1,2,0:T(8,128)S(1)}, u32[]{:S(2)}) copy-start(f32[8,8,4,256]{3,1,2,0:T(8,128)S(1)} %copy.275) | copy-start | bytes 786436
  49.7 26.9 %all-to-all-start.2 = ((bf16[16,64,1024]{2,1,0:T(8,128)(2,1)}), bf16[16,64,1024]{2,1,0:T(8,128)(2,1)S(1)}, u32[]{:S(2)}, u32[]{:S(2)}) async-start(bf16[16,64,1024]{2,1,0:T(8,128)(2,1)} %broadcast_in_dim.130), calls=%async_computation.2 | async-start | bytes 4194304 | tf_op jit(solution)/shard_map/all_to_all | solution.py:15
  91.5 35.7 %all-to-all-start.3 = ((bf16[16,64,1024]{2,1,0:T(8,128)(2,1)}), bf16[16,64,1024]{2,1,0:T(8,128)(2,1)S(1)}, u32[]{:S(2)}, u32[]{:S(2)}) async-start(bf16[16,64,1024]{2,1,0:T(8,128)(2,1)} %bitcast.401), calls=%async_computation.3 | async-start | bytes 4194304 | tf_op jit(solution)/shard_map/all_to_all | solution.py:36
  130.6 27.7 %all-to-all-start.4 = ((bf16[16,64,1024]{2,1,0:T(8,128)(2,1)}), bf16[16,64,1024]{2,1,0:T(8,128)(2,1)}, u32[]{:S(2)}, u32[]{:S(2)}) async-start(bf16[16,64,1024]{2,1,0:T(8,128)(2,1)} %broadcast_in_dim.131), calls=%async_computation.4 | async-start | bytes 4194304 | tf_op jit(solution)/shard_map/all_to_all | solution.py:15
  166.5 25.0 %all-to-all-start.5 = ((bf16[16,64,1024]{2,1,0:T(8,128)(2,1)}), bf16[16,64,1024]{2,1,0:T(8,128)(2,1)S(1)}, u32[]{:S(2)}, u32[]{:S(2)}) async-start(bf16[16,64,1024]{2,1,0:T(8,128)(2,1)} %bitcast.402), calls=%async_computation.5 | async-start | bytes 4194304 | tf_op jit(solution)/shard_map/all_to_all | solution.py:36
  192.2 22.5 %collective-permute-start = (bf16[64,1024]{1,0:T(8,128)(2,1)S(1)}, bf16[64,1024]{1,0:T(8,128)(2,1)S(1)}, u32[]{:S(2)}, u32[]{:S(2)}) collective-permute-start(bf16[64,1024]{1,0:T(8,128)(2,1)S(1)} %add_convert_fusion.8), channel_id=1, source_target_pairs={{0,64},{1,65},{2,66},{3,67},{4,68},{5,69},{6,70},{7,71},{8,72},{9,... | collective-permute-start | bytes 393224 | tf_op jit(solution)/shard_map/ppermute | solution.py:43
  325.2 29.1 %all-to-all-start.9 = ((bf16[16,64,1024]{2,1,0:T(8,128)(2,1)}), bf16[16,64,1024]{2,1,0:T(8,128)(2,1)S(1)}, u32[]{:S(2)}, u32[]{:S(2)}) async-start(bf16[16,64,1024]{2,1,0:T(8,128)(2,1)} %bitcast.399), calls=%async_computation.9 | async-start | bytes 4194304 | tf_op jit(solution)/shard_map/all_to_all | solution.py:36
  356.1 8.4 collective-permute-start.1
  364.5 74.8 %copy-start.36 = (bf16[64,1024]{1,0:T(8,128)(2,1)}, bf16[64,1024]{1,0:T(8,128)(2,1)S(1)}, u32[]{:S(2)}) copy-start(bf16[64,1024]{1,0:T(8,128)(2,1)S(1)} %collective-permute-done.1) | copy-start | bytes 393220
  472.7 29.1 %all-to-all-start.13 = ((bf16[16,64,1024]{2,1,0:T(8,128)(2,1)}), bf16[16,64,1024]{2,1,0:T(8,128)(2,1)S(1)}, u32[]{:S(2)}, u32[]{:S(2)}) async-start(bf16[16,64,1024]{2,1,0:T(8,128)(2,1)} %broadcast_in_dim.241), calls=%async_computation.13 | async-start | bytes 4194304 | tf_op jit(solution)/shard_map/all_to_all | solution.py:15
  542.2 27.9 %all-to-all-start.15 = ((bf16[16,64,1024]{2,1,0:T(8,128)(2,1)}), bf16[16,64,1024]{2,1,0:T(8,128)(2,1)S(1)}, u32[]{:S(2)}, u32[]{:S(2)}) async-start(bf16[16,64,1024]{2,1,0:T(8,128)(2,1)} %broadcast_in_dim.242), calls=%async_computation.15 | async-start | bytes 4194304 | tf_op jit(solution)/shard_map/all_to_all | solution.py:15
  617.5 7.7 collective-permute-start.2
  624.9 65.3 %copy-start.164 = (f32[64]{0:T(128)}, f32[64]{0:T(128)S(1)}, u32[]{:S(2)}) copy-start(f32[64]{0:T(128)S(1)} %compare_convert_fusion) | copy-start | bytes 772
  625.2 65.0 %copy-start.51 = (f32[8,8,4,256]{3,1,2,0:T(8,128)}, f32[8,8,4,256]{3,1,2,0:T(8,128)S(1)}, u32[]{:S(2)}) copy-start(f32[8,8,4,256]{3,1,2,0:T(8,128)S(1)} %copy.276) | copy-start | bytes 786436
  625.2 65.0 %copy-start.88 = (bf16[64,1024]{1,0:T(8,128)(2,1)}, bf16[64,1024]{1,0:T(8,128)(2,1)S(1)}, u32[]{:S(2)}) copy-start(bf16[64,1024]{1,0:T(8,128)(2,1)S(1)} %collective-permute-done.2) | copy-start | bytes 393220
  692.8 29.2 %all-to-all-start.19 = ((bf16[16,64,1024]{2,1,0:T(8,128)(2,1)}), bf16[16,64,1024]{2,1,0:T(8,128)(2,1)S(1)}, u32[]{:S(2)}, u32[]{:S(2)}) async-start(bf16[16,64,1024]{2,1,0:T(8,128)(2,1)} %broadcast_in_dim.244), calls=%async_computation.19 | async-start | bytes 4194304 | tf_op jit(solution)/shard_map/all_to_all | solution.py:15
  744.4 32.0 %all-to-all-start.20 = ((bf16[16,64,1024]{2,1,0:T(8,128)(2,1)}), bf16[16,64,1024]{2,1,0:T(8,128)(2,1)}, u32[]{:S(2)}, u32[]{:S(2)}) async-start(bf16[16,64,1024]{2,1,0:T(8,128)(2,1)} %bitcast.400), calls=%async_computation.20 | async-start | bytes 4194304 | tf_op jit(solution)/shard_map/all_to_all | solution.py:36
  776.3 32.5 %all-to-all-start.25 = ((bf16[16,64,1024]{2,1,0:T(8,128)(2,1)}), bf16[16,64,1024]{2,1,0:T(8,128)(2,1)}, u32[]{:S(2)}, u32[]{:S(2)}) async-start(bf16[16,64,1024]{2,1,0:T(8,128)(2,1)} %bitcast.397), calls=%async_computation.25 | async-start | bytes 4194304 | tf_op jit(solution)/shard_map/all_to_all | solution.py:36
  791.6 7.0 collective-permute-start.3
  810.5 31.8 %all-to-all-start.21 = ((bf16[16,64,1024]{2,1,0:T(8,128)(2,1)}), bf16[16,64,1024]{2,1,0:T(8,128)(2,1)}, u32[]{:S(2)}, u32[]{:S(2)}) async-start(bf16[16,64,1024]{2,1,0:T(8,128)(2,1)} %broadcast_in_dim.245), calls=%async_computation.21 | async-start | bytes 4194304 | tf_op jit(solution)/shard_map/all_to_all | solution.py:15
  848.3 32.4 %all-to-all-start.22 = ((bf16[16,64,1024]{2,1,0:T(8,128)(2,1)}), bf16[16,64,1024]{2,1,0:T(8,128)(2,1)}, u32[]{:S(2)}, u32[]{:S(2)}) async-start(bf16[16,64,1024]{2,1,0:T(8,128)(2,1)} %bitcast.398), calls=%async_computation.22 | async-start | bytes 4194304 | tf_op jit(solution)/shard_map/all_to_all | solution.py:36
  855.4 46.2 %reduce-scatter.11.cloned.1.call-start = ((), (), s32[]{:S(2)}) async-start(), calls=%async_computation.36 | async-start | bytes 655360 | tf_op jit(solution)/shard_map/reduce_scatter | solution.py:501
  864.5 46.1 %reduce-scatter.9.cloned.1.call-start = ((), (), s32[]{:S(2)}) async-start(), calls=%async_computation.35 | async-start | bytes 655360 | tf_op jit(solution)/shard_map/reduce_scatter | solution.py:498
  891.6 32.2 %all-to-all-start.23 = ((bf16[16,64,1024]{2,1,0:T(8,128)(2,1)}), bf16[16,64,1024]{2,1,0:T(8,128)(2,1)}, u32[]{:S(2)}, u32[]{:S(2)}) async-start(bf16[16,64,1024]{2,1,0:T(8,128)(2,1)} %broadcast_in_dim.246), calls=%async_computation.23 | async-start | bytes 4194304 | tf_op jit(solution)/shard_map/all_to_all | solution.py:15
  937.0 56.3 %all-to-all-start.24 = ((bf16[16,64,1024]{2,1,0:T(8,128)(2,1)}), bf16[16,64,1024]{2,1,0:T(8,128)(2,1)}, u32[]{:S(2)}, u32[]{:S(2)}) async-start(bf16[16,64,1024]{2,1,0:T(8,128)(2,1)} %bitcast.101), calls=%async_computation.24 | async-start | bytes 4194304 | tf_op jit(solution)/shard_map/all_to_all | solution.py:36
  944.0 24.6 %reduce-scatter.7.cloned.1.call-start = ((), (), s32[]{:S(2)}) async-start(), calls=%async_computation.34 | async-start | bytes 163840 | tf_op jit(solution)/shard_map/reduce_scatter | solution.py:495
  947.1 44.6 %reduce-scatter.5.cloned.1.call-start = ((), (), s32[]{:S(2)}) async-start(), calls=%async_computation.33 | async-start | bytes 491520 | tf_op jit(solution)/shard_map/reduce_scatter | solution.py:492
  1011.5 8.9 all-to-all-start.26
  1021.1 13.6 %all-to-all-start.28 = ((f32[16,1,1536]{2,1,0:T(1,128)}), f32[16,1,1536]{2,1,0:T(1,128)S(1)}, u32[]{:S(2)}, u32[]{:S(2)}) async-start(f32[16,1,1536]{2,1,0:T(1,128)} %broadcast_in_dim.249), calls=%async_computation.28 | async-start | bytes 196608 | tf_op jit(solution)/shard_map/all_to_all | solution.py:15
  1034.7 10.8 %all-to-all-start.27 = ((bf16[2,256,256]{2,0,1:T(2,128)(2,1)}), bf16[2,256,256]{2,0,1:T(2,128)(2,1)S(1)}, u32[]{:S(2)}, u32[]{:S(2)}) async-start(bf16[2,256,256]{2,0,1:T(2,128)(2,1)} %copy.259), calls=%async_computation.27 | async-start | bytes 524288 | tf_op jit(solution)/shard_map/all_to_all | solution.py:478
  (202 other events, 2241.5 us)
Sparse Core Ops, SparseCore 0:
  864.6 21.6 reduce-scatter.10
  889.3 21.2 reduce-scatter.8
  947.8 20.7 reduce-scatter.6
  971.5 20.1 reduce-scatter.4
where the time goes:
time: 1070 us; the launch traced here: 1050 us
  blocking collectives  428 us (40%)
  waiting for transfers between devices  223 us (21%)
  starting transfers between devices  117 us (11%)
  matrix products  104 us (10%)
  other arithmetic  84.4 us (8%)
  local copies, waits for them, and re-layouts  80 us (7%)
  between operations  17.6 us (2%)
    all_to_all x5, blocking collectives, from_everyone(): return lax.all_to_all(copies, axis, split_axis=0, concat_axis=0, tiled=True)  152 us
    all_to_all x5, blocking collectives, sum_at_owner(): lax.all_to_all(tiles, axis, split_axis=0, concat_axis=0, tiled=True)  151 us
    all_to_all x8, waiting for transfers between devices, from_everyone(): return lax.all_to_all(copies, axis, split_axis=0, concat_axis=0, tiled=True)  87.7 us
    all_to_all x7, waiting for transfers between devices, sum_at_owner(): lax.all_to_all(tiles, axis, split_axis=0, concat_axis=0, tiled=True)  55.4 us
    all_to_all x7, starting transfers between devices, sum_at_owner(): lax.all_to_all(tiles, axis, split_axis=0, concat_axis=0, tiled=True)  47.4 us
    all_to_all x8, starting transfers between devices, from_everyone(): return lax.all_to_all(copies, axis, split_axis=0, concat_axis=0, tiled=True)  42.9 us
    dot_general x12, matrix products, weight_grad(): lax.dot_general(gathered_in, gathered_out, (((0,), (0,)), ((), ())), pref...  28.4 us
    ppermute x4, waiting for transfers between devices, shifted(): return lax.ppermute(shard, axis, pairs)  27.3 us
  transfers between devices with their start and end apart: 26, of which 19 were waited for; matrix products, arithmetic and copies ran while one was open for 11% of the time, Pallas kernels for 0%

commit v1 on v0

v1 whole, which is shorter than its diff:
```python
import jax
import jax.numpy as jnp
from jax import lax
from jax.experimental import pallas as pl
from jax.experimental.pallas import tpu as pltpu
from jax.sharding import Mesh
from jax.sharding import PartitionSpec as P

HD = 64
norm_eps = 1e-06
bf16 = jnp.bfloat16
f32 = jnp.float32
SCALE = HD ** (-0.5)


def shift(v, axis, by):
    return lax.ppermute(v, axis, [(i, (i + by) % 4) for i in range(4)])


def gather4(v, axis):
    far = shift(v, axis, 2)
    return [v, shift(v, axis, 1), shift(v, axis, 3), far]


def scatter4(parts, axis):
    far = shift(parts[3], axis, 2)
    return [parts[0], shift(parts[1], axis, 3), shift(parts[2], axis, 1), far]


def sum4(parts):
    a, b, c, d = [p.astype(f32) for p in parts]
    return (a + b) + (c + d)


def swap_core(v):
    return lax.ppermute(v, "section", [(0, 1), (1, 0)])


def swap_pair(v):
    return lax.ppermute(v, "row", [(0, 1), (1, 0), (2, 3), (3, 2)])


def gather_tokens(rows):
    return jnp.concatenate(gather4(rows, "z"), axis=0)


def scatter_tokens(partial):
    low = partial.astype(bf16)
    n = low.shape[0] // 4
    return sum4(scatter4([low[i * n : (i + 1) * n] for i in range(4)], "z"))


def dot(a, b):
    return jnp.dot(a, b, preferred_element_type=f32)


def dot_t(a, b):
    return lax.dot_general(a, b, (((1,), (1,)), ((), ())), preferred_element_type=f32)


def t_dot(a, b):
    return lax.dot_general(a, b, (((0,), (0,)), ((), ())), preferred_element_type=f32)


def norm_local(features, gain, bias):
    center = jnp.mean(features, axis=-1, keepdims=True)
    offset = features - center
    spread = jnp.mean(offset * offset, axis=-1, keepdims=True)
    inverse = lax.rsqrt(spread + norm_eps)
    scaled = offset * inverse
    return scaled * gain + bias, scaled, inverse


def norm_back(upstream, scaled, inverse, gain):
    weighted = upstream * gain
    first = jnp.mean(weighted, axis=-1, keepdims=True)
    second = jnp.mean(weighted * scaled, axis=-1, keepdims=True)
    result = inverse * (weighted - first - scaled * second)
    return result, jnp.sum(upstream * scaled, axis=0), jnp.sum(upstream, axis=0)


def gelu_both(v):
    cdf = 0.5 * (1.0 + lax.erf(v * (0.5**0.5)))
    density = jnp.exp(-0.5 * v * v) * 0.3989422804014327
    return (v * cdf).astype(bf16), cdf + v * density


def attend_kernel(q_ref, own_ref, core_ref, pair_ref, both_ref, o_ref, lt_ref):
    q = q_ref[...]
    kv = jnp.concatenate([own_ref[...], core_ref[...], pair_ref[...], both_ref[...]], axis=0)
    s = dot_t(q, kv) * SCALE
    peak = jnp.max(s, axis=-1, keepdims=True)
    raised = jnp.exp(s - peak)
    total = jnp.sum(raised, axis=-1, keepdims=True)
    low = (raised * (1.0 / total)).astype(bf16)
    o = dot(low, kv)
    upper = lax.broadcasted_iota(jnp.int32, o.shape, 1) >= HD
    o_ref[...] = jnp.where(upper, o, 0.0).astype(bf16)
    lt_ref[...] = jnp.broadcast_to(peak + jnp.log(total), lt_ref.shape)


def attend(q, kvs):
    tokens, width = q.shape
    spec = pl.BlockSpec((tokens, 128), lambda h: (0, h))
    return pl.pallas_call(
        attend_kernel,
        grid=(width // 128,),
        in_specs=[spec] * 5,
        out_specs=[spec, spec],
        out_shape=[
            jax.ShapeDtypeStruct((tokens, width), bf16),
            jax.ShapeDtypeStruct((tokens, width), f32),
        ],
        compiler_params=pltpu.CompilerParams(vmem_limit_bytes=32 * 2**20),
        cost_estimate=pl.CostEstimate(flops=4 * 2 * 2 * 256 * 1024 * 128, bytes_accessed=2**21, transcendentals=2**20),
    )(q, *kvs)


def attend_back_kernel(
    q_ref, own_ref, core_ref, pair_ref, both_ref, g_ref, lt_ref, dq_ref, down_ref, dcore_ref, dpair_ref, dboth_ref
):
    q = q_ref[...]
    n = q.shape[0]
    upper = lax.broadcasted_iota(jnp.int32, q.shape, 1) >= HD
    g = jnp.where(upper, g_ref[...], jnp.zeros_like(q))
    kv = jnp.concatenate([own_ref[...], core_ref[...], pair_ref[...], both_ref[...]], axis=0)
    s = dot_t(q, kv) * SCALE
    probs = jnp.exp(s - lt_ref[:, 0:1])
    grad_probs = dot_t(g, kv)
    along = jnp.sum(probs * grad_probs, axis=-1, keepdims=True)
    ds = (probs * (grad_probs - along)).astype(bf16)
    low = probs.astype(bf16)
    dq = dot(ds, kv) * SCALE
    dq_ref[...] = jnp.where(upper, 0.0, dq).astype(bf16)
    dkv = t_dot(ds, q) * SCALE + t_dot(low, g)
    down_ref[...] = dkv[0:n].astype(down_ref.dtype)
    dcore_ref[...] = dkv[n : 2 * n].astype(dcore_ref.dtype)
    dpair_ref[...] = dkv[2 * n : 3 * n].astype(dpair_ref.dtype)
    dboth_ref[...] = dkv[3 * n :].astype(dboth_ref.dtype)


def attend_back(q, kvs, g, lt):
    tokens, width = q.shape
    spec = pl.BlockSpec((tokens, 128), lambda h: (0, h))
    return pl.pallas_call(
        attend_back_kernel,
        grid=(width // 128,),
        in_specs=[spec] * 7,
        out_specs=[spec] * 5,
        out_shape=[
            jax.ShapeDtypeStruct((tokens, width), bf16),
            jax.ShapeDtypeStruct((tokens, width), f32),
            jax.ShapeDtypeStruct((tokens, width), bf16),
            jax.ShapeDtypeStruct((tokens, width), f32),
            jax.ShapeDtypeStruct((tokens, width), bf16),
        ],
        compiler_params=pltpu.CompilerParams(vmem_limit_bytes=40 * 2**20),
        cost_estimate=pl.CostEstimate(flops=4 * 5 * 2 * 256 * 1024 * 128, bytes_accessed=2**22, transcendentals=2**20),
    )(q, *kvs, g, lt)


def forward(u, w):
    vec = w["vec"]
    lower = (jnp.arange(512) % 128) < HD
    n1, scaled1, inv1 = norm_local(u, vec[0], vec[1])
    x = gather_tokens(n1.astype(bf16))
    kv = (dot(x, w["kv"]) + w["kv_bias"]).astype(bf16)
    q = (jnp.where(lower, dot(x, w["qp"]), 0.0) + w["q_bias"]).astype(bf16)
    kv_pair = swap_pair(kv)
    kvs = (kv, swap_core(kv), kv_pair, swap_core(kv_pair))
    o, lt = attend(q, kvs)
    attended = scatter_tokens(dot_t(o, w["qp"])) + vec[2]
    hidden = u + vec[3] * attended
    n2, scaled2, inv2 = norm_local(hidden, vec[4], vec[5])
    x2 = gather_tokens(n2.astype(bf16))
    a_own, da_own = gelu_both(dot(x2, w["in_own"]) + w["in_bias_own"])
    a_oth, da_oth = gelu_both(dot(x2, w["in_oth"]) + w["in_bias_oth"])
    contracted = scatter_tokens(dot_t(a_own, w["out_own"]) + dot_t(a_oth, w["out_oth"])) + vec[6]
    out = hidden + vec[7] * contracted
    return out, (scaled1, inv1, x, kvs, q, o, lt, attended, scaled2, inv2, x2, a_own, da_own, a_oth, da_oth, contracted)


def both_cores(mine, sent):
    return jnp.concatenate([mine, swap_core(sent)], axis=0)


def backward(g, saved, w, first):
    scaled1, inv1, x, kvs, q, o, lt, attended, scaled2, inv2, x2, a_own, da_own, a_oth, da_oth, contracted = saved
    vec = w["vec"]
    grad_mlp_scale = jnp.sum(g * contracted, axis=0)
    gc = (g * vec[7]).astype(bf16)
    grad_outer_bias = jnp.sum(gc.astype(f32), axis=0)
    gcs = gather_tokens(gc)
    ge_own = (dot(gcs, w["out_own"]) * da_own).astype(bf16)
    ge_oth = (dot(gcs, w["out_oth"]) * da_oth).astype(bf16)
    grad_second = scatter_tokens(dot_t(ge_own, w["in_own"]) + dot_t(ge_oth, w["in_oth"]))
    d_out = t_dot(both_cores(gcs, gcs), both_cores(a_own, a_oth)).astype(bf16)
    ge_both = both_cores(ge_own, ge_oth)
    d_in = t_dot(both_cores(x2, x2), ge_both).astype(bf16)
    in_bias_sum = jnp.sum(ge_both.astype(f32), axis=0)
    back, grad_gain2, grad_bias2 = norm_back(grad_second, scaled2, inv2, vec[4])
    grad_hidden = g + back
    grad_attn_scale = jnp.sum(grad_hidden * attended, axis=0)
    ga = (grad_hidden * vec[3]).astype(bf16)
    grad_proj_bias = jnp.sum(ga.astype(f32), axis=0)
    gas = gather_tokens(ga)
    gz = dot(gas, w["qp"]).astype(bf16)
    dq, d_own, d_core, d_pair, d_both = attend_back(q, kvs, gz, lt)
    pair_sum = (d_pair + swap_core(d_both).astype(f32)).astype(bf16)
    dkv = (d_own + swap_core(d_core).astype(f32) + swap_pair(pair_sum).astype(f32)).astype(bf16)
    grad_normed = scatter_tokens(dot_t(dkv, w["kv"]) + dot_t(dq, w["qp"]))
    m1 = both_cores(jnp.where(first, dkv, dq), jnp.where(first, dq, dkv))
    m2 = jnp.where(first, jnp.zeros((), bf16), both_cores(o, o))
    d_att = (t_dot(both_cores(x, x), m1) + t_dot(both_cores(gas, gas), m2)).astype(bf16)
    att_bias_sum = jnp.sum(m1.astype(f32), axis=0)
    back, grad_gain1, grad_bias1 = norm_back(grad_normed, scaled1, inv1, vec[0])
    grad_u = grad_hidden + back
    rows = jnp.stack(
        [grad_gain1, grad_bias1, grad_proj_bias, grad_attn_scale, grad_gain2, grad_bias2, grad_outer_bias, grad_mlp_scale]
    )
    cols = jnp.concatenate([att_bias_sum.reshape(4, 128), in_bias_sum.reshape(4, 128)], axis=1)
    return grad_u, (d_att, d_in, d_out), rows, cols


def gather_block(block):
    rows = jnp.concatenate(gather4(block, "row"), axis=0)
    return gather4(rows, "x")


def side_by_side(tiles, at, width):
    return jnp.concatenate([t[:, at : at + width] for t in tiles], axis=1)


def layer_weights(half_att, half_ffn, vec_y, vec_x, first):
    att = side_by_side(gather_block(half_att), 0, 128)
    att_far = swap_core(att)
    tiles = gather_block(half_ffn)
    in_own, out_own = side_by_side(tiles, 0, 128), side_by_side(tiles, 128, 128)
    zeros = jnp.zeros((HD,), f32)
    kv_bias = jnp.concatenate([t for v in vec_x for t in (zeros, v[HD : 2 * HD])])
    q_bias = jnp.concatenate([t for v in vec_x for t in (v[:HD], zeros)])
    low = jnp.concatenate([v[128:256] for v in vec_x])
    high = jnp.concatenate([v[256:384] for v in vec_x])
    return {
        "vec": vec_y,
        "kv": jnp.where(first, att, att_far),
        "qp": jnp.where(first, att_far, att),
        "in_own": in_own,
        "out_own": out_own,
        "in_oth": swap_core(in_own),
        "out_oth": swap_core(out_own),
        "kv_bias": kv_bias,
        "q_bias": q_bias,
        "in_bias_own": jnp.where(first, low, high),
        "in_bias_oth": jnp.where(first, high, low),
    }


def reduce_block(d, count):
    parts = [jnp.concatenate([m[:, i * 128 : (i + 1) * 128] for m in d], axis=1) for i in range(4)]
    summed = sum4(scatter4(parts, "x")).astype(bf16)
    n = summed.shape[0] // 4
    return sum4(scatter4([summed[i * n : (i + 1) * n] for i in range(4)], "row"))


def local(
    block_input,
    cotangent,
    images_used,
    norm1_gain,
    norm1_bias,
    qkv_weight,
    query_bias,
    value_bias,
    proj_weight,
    proj_bias,
    attn_scale,
    norm2_gain,
    norm2_bias,
    inner_weight,
    inner_bias,
    outer_weight,
    outer_bias,
    mlp_scale,
):
    first = lax.axis_index("section") == 0
    y = lax.axis_index("row")

    qkv = qkv_weight[0]
    half0_att = qkv[:, HD:]
    half1_att = jnp.concatenate([qkv[:, :HD], proj_weight[0].T], axis=1)
    outer_t = outer_weight[0].T
    half0_ffn = jnp.concatenate([inner_weight[0][:, :128], outer_t[:, :128]], axis=1)
    half1_ffn = jnp.concatenate([inner_weight[0][:, 128:], outer_t[:, 128:]], axis=1)

    def split_layers(h0, h1):
        kept, got = jnp.where(first, h0, h1), swap_core(jnp.where(first, h1, h0))
        return jnp.where(first, kept, got), jnp.where(first, got, kept)

    att0, att1 = split_layers(half0_att, half1_att)
    ffn0, ffn1 = split_layers(half0_ffn, half1_ffn)

    def both_layers(own):
        got = swap_core(own)
        return jnp.stack([jnp.where(first, own, got), jnp.where(first, got, own)])

    vec_y = both_layers(
        jnp.concatenate(
            [norm1_gain, norm1_bias, proj_bias, attn_scale, norm2_gain, norm2_bias, outer_bias, mlp_scale], axis=0
        )
    )
    vec_x = both_layers(jnp.concatenate([query_bias[0], value_bias[0], inner_bias[0]]))
    vec_y = jnp.concatenate(gather4(vec_y, "row"), axis=2)
    vec_x = gather4(vec_x, "x")

    paired = jnp.stack([block_input, cotangent]).reshape(2, 4, 2, 64, 256)
    paired = jnp.where(first, paired[:, :, 0], paired[:, :, 1])
    chunk = [lax.dynamic_index_in_dim(paired, (y + k) % 4, 1, keepdims=False) for k in (0, 3, 1, 2)]
    got = scatter4(chunk, "row")
    tokens = jnp.concatenate([got[0], got[2], got[1], got[3]], axis=2).astype(f32)

    w0 = layer_weights(att0, ffn0, vec_y[0], [v[0] for v in vec_x], first)
    w1 = layer_weights(att1, ffn1, vec_y[1], [v[1] for v in vec_x], first)

    used = jnp.where(y < 2, images_used[0], images_used[1])
    live = (lax.axis_index("x") < used).astype(f32)

    out0, saved0 = forward(tokens[0], w0)
    out1, saved1 = forward(out0.astype(bf16).astype(f32), w1)
    final = (live * out1).astype(bf16)
    back1, d1, rows1, cols1 = backward(live * tokens[1], saved1, w1, first)
    back0, d0, rows0, cols0 = backward(back1.astype(bf16).astype(f32), saved0, w0, first)
    grad_in = back0.astype(bf16)

    own = jnp.where(first, grad_in, final)
    got = swap_core(jnp.where(first, final, grad_in))
    edge = jnp.concatenate([jnp.where(first, own, got), jnp.where(first, got, own)], axis=0)
    got = scatter4([edge[:, i * 256 : (i + 1) * 256] for i in range(4)], "row")
    edge = jnp.stack([got[0], got[1], got[3], got[2]])
    edge = lax.dynamic_slice_in_dim(jnp.concatenate([edge, edge]), (4 - y) % 4, 4, 0)
    edge = edge.reshape(1, 2, 256, 256).astype(f32)

    def own_layer(l0, l1):
        got = swap_core(jnp.where(first, l1, l0))
        mine = jnp.where(first, l0, l1)
        return jnp.where(first, mine, got), jnp.where(first, got, mine)

    d_ffn = own_layer(*[reduce_block(d[1:], 2).astype(bf16) for d in (d0, d1)])
    d_att = own_layer(*[reduce_block(d[:1], 1).astype(bf16) for d in (d0, d1)])
    h0, h1 = [h.astype(f32) for h in d_att]
    grad_qkv = jnp.concatenate([h1[:, :HD], h0], axis=1)
    grad_proj = h1[:, HD:].T
    h0, h1 = [h.astype(f32) for h in d_ffn]
    grad_inner = jnp.concatenate([h0[:, :128], h1[:, :128]], axis=1)
    grad_outer = jnp.concatenate([h0[:, 128:], h1[:, 128:]], axis=1).T

    cols = jnp.stack([cols0, cols1], axis=1)
    cols = sum4(scatter4([cols[i] for i in range(4)], "x"))
    cols = sum4(gather4(cols, "row"))
    h0, h1 = own_layer(cols[0], cols[1])
    grad_query_bias, grad_value_bias = h1[:HD], h0[HD:128]
    grad_inner_bias = jnp.concatenate([h0[128:], h1[128:]])

    rows = jnp.where(first, rows0, rows1) + swap_core(jnp.where(first, rows1, rows0))
    rows = sum4(scatter4([rows[:, i * 256 : (i + 1) * 256] for i in range(4)], "row"))
    rows = sum4(gather4(rows, "x"))
    rows = sum4(gather4(rows, "z"))

    return (
        edge,
        rows[0][None],
        rows[1][None],
        grad_qkv[None],
        grad_query_bias[None],
        grad_value_bias[None],
        grad_proj[None],
        rows[2][None],
        rows[3][None],
        rows[4][None],
        rows[5][None],
        grad_inner[None],
        grad_inner_bias[None],
        grad_outer[None],
        rows[6][None],
        rows[7][None],
    )


def solution(mesh):
    grid = Mesh(mesh.devices.reshape(2, 4, 4, 4), ("section", "row", "x", "z"))
    col = ("x", "z")
    by_row = P("section", "row")
    by_col = P("section", col)
    matrix = P("section", "row", col)
    matrix_t = P("section", col, "row")
    return jax.shard_map(
        local,
        mesh=grid,
        in_specs=(
            P(None, col, "row"),
            P(None, col, "row"),
            P(),
            by_row,
            by_row,
            matrix,
            by_col,
            by_col,
            matrix_t,
            by_row,
            by_row,
            by_row,
            by_row,
            matrix,
            by_col,
            matrix_t,
            by_row,
            by_row,
        ),
        out_specs=(
            P("section", None, col, "row"),
            by_row,
            by_row,
            matrix,
            by_col,
            by_col,
            matrix_t,
            by_row,
            by_row,
            by_row,
            by_row,
            matrix,
            by_col,
            matrix_t,
            by_row,
            by_row,
        ),
        check_vma=False,
    )
```

time: 1070 us -> 492 us (0.46)
  blocking collectives: 428 us -> 0 us
  starting transfers between devices: 117 us -> 223 us
  matrix products: 104 us -> 24.6 us
  local copies, waits for them, and re-layouts: 80 us -> 18.8 us
  waiting for transfers between devices: 223 us -> 165 us
  other arithmetic: 84.4 us -> 30.3 us
  Pallas kernels: 0 us -> 17.4 us
  between operations: 17.6 us -> 4.57 us
    all_to_all x11 -> x0, blocking collectives: 322 us -> none  [the longest x5 152 us: from_everyone(): return lax.all_to_all(copies, axis, split_axis=0, concat_axis=0, tiled=True)]
    ppermute x4 -> x166, starting transfers between devices: 14.5 us -> 223 us  [the longest x123 131 us: shift(): return lax.ppermute(v, axis, [(i, (i + by) % 4) for i in range(4)])]
    all_to_all x18 -> x0, waiting for transfers between devices: 152 us -> none  [the longest x8 87.7 us: from_everyone(): return lax.all_to_all(copies, axis, split_axis=0, concat_axis=0, tiled=True)]
    ppermute x4 -> x166, waiting for transfers between devices: 27.3 us -> 165 us  [the longest x123 147 us: shift(): return lax.ppermute(v, axis, [(i, (i + by) % 4) for i in range(4)])]
    all_to_all x18 -> x0, starting transfers between devices: 101 us -> none  [the longest x7 47.4 us: sum_at_owner(): lax.all_to_all(tiles, axis, split_axis=0, concat_axis=0, tiled=True)]
    all_gather x12 -> x0, blocking collectives: 94.3 us -> none  [the longest x1 11.2 us: local(): lax.all_gather(weights[12], 'row', axis=1, tiled=True)]
    dot_general x54 -> x36, matrix products: 104 us -> 24.6 us  [the longest x8 9.27 us: t_dot(): lax.dot_general(a, b, (((0,), (0,)), ((), ())), preferred_element_type=f32)]
    reduce_scatter x4 -> x0, waiting for transfers between devices: 44.4 us -> none  [the longest x1 21.7 us: local(): lax.psum_scatter(wide_totals[2].astype(jnp.bfloat16), 'row', scatter_dime...]
  transfers between devices with their start and end apart: 26 -> 166, of which waited for: 19 -> 70; matrix products, arithmetic and copies ran while one was open for 11% -> 14% of each run, Pallas kernels for 0% -> 4%
where the time goes in v1:
time: 492 us; the launch traced here: 483 us
  starting transfers between devices  223 us (45%)
  waiting for transfers between devices  165 us (34%)
  other arithmetic  30.3 us (6%)
  matrix products  24.6 us (5%)
  local copies, waits for them, and re-layouts  18.8 us (4%)
  Pallas kernels  17.4 us (4%)
    ppermute x123, waiting for transfers between devices, shift(): return lax.ppermute(v, axis, [(i, (i + by) % 4) for i in range(4)])  147 us
    ppermute x123, starting transfers between devices, shift(): return lax.ppermute(v, axis, [(i, (i + by) % 4) for i in range(4)])  131 us
    ppermute x39, starting transfers between devices, swap_core(): return lax.ppermute(v, 'section', [(0, 1), (1, 0)])  86.8 us
    ppermute x4, waiting for transfers between devices, swap_pair(): return lax.ppermute(v, 'row', [(0, 1), (1, 0), (2, 3), (3, 2)])  15.5 us
    pallas_call x2, Pallas kernels, attend_back(): pl.pallas_call(attend_back_kernel, grid=(width // 128,), in_specs=[spec]...  10.1 us
  transfers between devices with their start and end apart: 166, of which 70 were waited for; matrix products, arithmetic and copies ran while one was open for 14% of the time, Pallas kernels for 4%

profile of v1, /device:TPU:1, one launch (start us, length us, event | category | flops | bytes accessed | tf_op | source)
XLA Modules:
  0.0 483.0 jit_solution(15633478926433343226)
XLA Ops:
  65.9 4.0 collective-permute-done.51
  71.6 12.1 %collective-permute-start.157 = (bf16[256,1024]{1,0:T(8,128)(2,1)S(1)}, bf16[256,1024]{1,0:T(8,128)(2,1)S(1)}, u32[]{:S(2)}, u32[]{:S(2)}) collective-permute-start(bf16[256,1024]{1,0:T(8,128)(2,1)S(1)} %pad_maximum_fusion.10), channel_id=1, source_target_pairs={{0,64},{64,0},{1,65},{65,1},{2,66},{66,2},{3,67},{67,3},{4,68},{68... | collective-permute-start | bytes 1572872 | tf_op jit(solution)/shard_map/ppermute | solution.py:36
  91.7 7.6 %collective-permute-done.37 = bf16[1024,256]{0,1:T(8,128)(2,1)S(1)} collective-permute-done((bf16[1024,256]{0,1:T(8,128)(2,1)S(1)}, bf16[1024,256]{0,1:T(8,128)(2,1)S(1)}, u32[]{:S(2)}, u32[]{:S(2)}) %collective-permute-start.37) | collective-permute-done | bytes 524320 | tf_op jit(solution)/shard_map/ppermute | solution.py:17
  99.3 5.0 %collective-permute-start.17 = (bf16[1024,512]{0,1:T(8,128)(2,1)S(1)}, bf16[1024,512]{0,1:T(8,128)(2,1)S(1)}, u32[]{:S(2)}, u32[]{:S(2)}) collective-permute-start(bf16[1024,512]{0,1:T(8,128)(2,1)S(1)} %pad_maximum_fusion), channel_id=1, source_target_pairs={{0,64},{64,0},{1,65},{65,1},{2,66},{66,2},{3,67},{67,3},{4,68},{68... | collective-permute-start | bytes 3145736 | tf_op jit(solution)/shard_map/ppermute | solution.py:36
  104.3 4.2 collective-permute-done.36
  113.7 8.2 %collective-permute-done.67 = bf16[1024,256]{0,1:T(8,128)(2,1)S(1)} collective-permute-done((bf16[1024,256]{0,1:T(8,128)(2,1)S(1)}, bf16[1024,256]{0,1:T(8,128)(2,1)S(1)}, u32[]{:S(2)}, u32[]{:S(2)}) %collective-permute-start.67) | collective-permute-done | bytes 524320 | tf_op jit(solution)/shard_map/ppermute | solution.py:17
  121.8 5.0 %collective-permute-start.38 = (bf16[1024,512]{0,1:T(8,128)(2,1)S(1)}, bf16[1024,512]{0,1:T(8,128)(2,1)S(1)}, u32[]{:S(2)}, u32[]{:S(2)}) collective-permute-start(bf16[1024,512]{0,1:T(8,128)(2,1)S(1)} %pad_maximum_fusion.1), channel_id=1, source_target_pairs={{0,64},{64,0},{1,65},{65,1},{2,66},{66,2},{3,67},{67,3},{4,68},{68... | collective-permute-start | bytes 3145736 | tf_op jit(solution)/shard_map/ppermute | solution.py:36
  137.3 3.7 shard_map.297
  148.3 3.8 collective-permute-done.26
  171.9 4.3 collective-permute-done.41
  178.4 4.5 collective-permute-done.45
  189.0 5.1 %collective-permute-done.54.pair_ref = bf16[256,512]{1,0:T(8,128)(2,1)S(1)} collective-permute-done((bf16[256,512]{1,0:T(8,128)(2,1)S(1)}, bf16[256,512]{1,0:T(8,128)(2,1)S(1)}, u32[]{:S(2)}, u32[]{:S(2)}) %collective-permute-start.54) | collective-permute-done | bytes 262176 | tf_op jit(solution)/shard_map/ppermute | solution.py:40
  196.8 3.7 shard_map.298
  246.4 3.7 collective-permute-start.156
  251.8 5.1 %shard_map.299 = (bf16[256,512]{1,0:T(8,128)(2,1)S(1)}, f32[256,512]{1,0:T(8,128)S(1)}, bf16[256,512]{1,0:T(8,128)(2,1)S(1)}, f32[256,512]{1,0:T(8,128)S(1)}, bf16[256,512]{1,0:T(8,128)(2,1)S(1)}) custom-call(bf16[256,512]{1,0:T(8,128)(2,1)S(1)} %fusion.15.q_ref, bf16[256,512]{1,0:T(8,128)(2,1)S(1)} %fusion.9.own_ref, ...), custom_call_target="tpu_custom_call" | custom-call | flops 1342177280 | bytes 4194304 | tf_op jit(solution)/shard_map/pallas_call | solution.py:145
  264.2 5.9 %collective-permute-done.81 = bf16[256,512]{1,0:T(8,128)(2,1)S(1)} collective-permute-done((bf16[256,512]{1,0:T(8,128)(2,1)S(1)}, bf16[256,512]{1,0:T(8,128)(2,1)S(1)}, u32[]{:S(2)}, u32[]{:S(2)}) %collective-permute-start.81) | collective-permute-done | bytes 262176 | tf_op jit(solution)/shard_map/ppermute | solution.py:40
  276.3 4.1 collective-permute-done.83
  284.9 3.8 collective-permute-done.160
  288.6 5.0 %collective-permute-start.86 = (bf16[64,1024]{1,0:T(8,128)(2,1)S(1)}, bf16[64,1024]{1,0:T(8,128)(2,1)S(1)}, u32[]{:S(2)}, u32[]{:S(2)}) collective-permute-start(bf16[64,1024]{1,0:T(8,128)(2,1)S(1)} %get-tuple-element.83), channel_id=1, source_target_pairs={{0,3},{1,0},{2,1},{3,2},{4,7},{5,4},{6,5},{7,6},{8,11},{9,8},{10,9... | collective-permute-start | bytes 393224 | tf_op jit(solution)/shard_map/ppermute | solution.py:17
  301.3 6.7 %collective-permute-start.118 = (bf16[256,512]{1,0:T(8,128)(2,1)S(1)}, bf16[256,512]{1,0:T(8,128)(2,1)S(1)}, u32[]{:S(2)}, u32[]{:S(2)}) collective-permute-start(bf16[256,512]{1,0:T(8,128)(2,1)S(1)} %broadcast_select_fusion.10), channel_id=1, source_target_pairs={{0,64},{64,0},{1,65},{65,1},{2,66},{66,2},{3,67},{67,3},{4,68},{68... | collective-permute-start | bytes 786440 | tf_op jit(solution)/shard_map/ppermute | solution.py:36
  326.3 4.4 collective-permute-start.102
  330.7 4.1 collective-permute-done.122
  335.7 4.1 collective-permute-done.91
  345.1 4.4 collective-permute-start.148
  349.9 5.1 %shard_map.300 = (bf16[256,512]{1,0:T(8,128)(2,1)S(1)}, f32[256,512]{1,0:T(8,128)S(1)}, bf16[256,512]{1,0:T(8,128)(2,1)S(1)}, f32[256,512]{1,0:T(8,128)S(1)}, bf16[256,512]{1,0:T(8,128)(2,1)S(1)}) custom-call(bf16[256,512]{1,0:T(8,128)(2,1)S(1)} %fusion.14.q_ref, bf16[256,512]{1,0:T(8,128)(2,1)S(1)} %fusion.8.own_ref, ...), custom_call_target="tpu_custom_call" | custom-call | flops 1342177280 | bytes 4194304 | tf_op jit(solution)/shard_map/pallas_call | solution.py:145
  362.5 4.2 collective-permute-done.96
  407.8 6.1 %collective-permute-start.128 = (bf16[256,512]{1,0:T(8,128)(2,1)S(1)}, bf16[256,512]{1,0:T(8,128)(2,1)S(1)}, u32[]{:S(2)}, u32[]{:S(2)}) collective-permute-start(bf16[256,512]{1,0:T(8,128)(2,1)S(1)} %broadcast_select_fusion.8), channel_id=1, source_target_pairs={{0,64},{64,0},{1,65},{65,1},{2,66},{66,2},{3,67},{67,3},{4,68},{68... | collective-permute-start | bytes 786440 | tf_op jit(solution)/shard_map/ppermute | solution.py:36
  431.0 3.9 collective-permute-start.146
  439.8 3.6 collective-permute-done.105
  443.6 4.2 collective-permute-done.106
  455.6 5.0 %collective-permute-start.165 = (bf16[256,256]{0,1:T(8,128)(2,1)S(1)}, bf16[256,256]{0,1:T(8,128)(2,1)S(1)}, u32[]{:S(2)}, u32[]{:S(2)}) collective-permute-start(bf16[256,256]{0,1:T(8,128)(2,1)S(1)} %get-tuple-element.77), channel_id=1, source_target_pairs={{0,64},{64,0},{1,65},{65,1},{2,66},{66,2},{3,67},{67,3},{4,68},{68... | collective-permute-start | bytes 393224 | tf_op jit(solution)/shard_map/ppermute | solution.py:36
  461.8 8.8 %collective-permute-done.132 = bf16[1024,128]{0,1:T(8,128)(2,1)S(1)} collective-permute-done((bf16[1024,128]{0,1:T(8,128)(2,1)S(1)}, bf16[1024,128]{0,1:T(8,128)(2,1)S(1)}, u32[]{:S(2)}, u32[]{:S(2)}) %collective-permute-start.132) | collective-permute-done | bytes 262176 | tf_op jit(solution)/shard_map/ppermute | solution.py:17
  (668 shorter events, 315.3 us)
Async XLA Ops:
  5.5 23.2 %collective-permute-start.10 = (bf16[256,128]{0,1:T(8,128)(2,1)S(1)}, bf16[256,128]{0,1:T(8,128)(2,1)S(1)}, u32[]{:S(2)}, u32[]{:S(2)}) collective-permute-start(bf16[256,128]{0,1:T(8,128)(2,1)S(1)} %broadcast_select_fusion.26), channel_id=1, source_target_pairs={{0,64},{64,0},{1,65},{65,1},{2,66},{66,2},{3,67},{67,3},{4,68},{68... | collective-permute-start | bytes 196616 | tf_op jit(solution)/shard_map/ppermute | solution.py:36
  8.0 27.1 %collective-permute-start.31 = (bf16[256,256]{0,1:T(8,128)(2,1)S(1)}, bf16[256,256]{0,1:T(8,128)(2,1)S(1)}, u32[]{:S(2)}, u32[]{:S(2)}) collective-permute-start(bf16[256,256]{0,1:T(8,128)(2,1)S(1)} %broadcast_select_fusion.16), channel_id=1, source_target_pairs={{0,64},{64,0},{1,65},{65,1},{2,66},{66,2},{3,67},{67,3},{4,68},{68... | collective-permute-start | bytes 393224 | tf_op jit(solution)/shard_map/ppermute | solution.py:36
  61.7 22.0 %collective-permute-start.15 = (bf16[1024,128]{0,1:T(8,128)(2,1)S(1)}, bf16[1024,128]{0,1:T(8,128)(2,1)S(1)}, u32[]{:S(2)}, u32[]{:S(2)}) collective-permute-start(bf16[1024,128]{0,1:T(8,128)(2,1)S(1)} %pad_maximum_fusion.31), channel_id=1, source_target_pairs={{0,12},{4,0},{8,4},{12,8},{1,13},{5,1},{9,5},{13,9},{2,14},{6,2},{... | collective-permute-start | bytes 786440 | tf_op jit(solution)/shard_map/ppermute | solution.py:17
  63.7 22.8 %collective-permute-start.50 = (bf16[1024,128]{0,1:T(8,128)(2,1)S(1)}, bf16[1024,128]{0,1:T(8,128)(2,1)S(1)}, u32[]{:S(2)}, u32[]{:S(2)}) collective-permute-start(bf16[1024,128]{0,1:T(8,128)(2,1)S(1)} %pad_maximum_fusion.32), channel_id=1, source_target_pairs={{0,12},{4,0},{8,4},{12,8},{1,13},{5,1},{9,5},{13,9},{2,14},{6,2},{... | collective-permute-start | bytes 786440 | tf_op jit(solution)/shard_map/ppermute | solution.py:17
  65.8 18.0 %collective-permute-start.14 = (bf16[1024,128]{0,1:T(8,128)(2,1)S(1)}, bf16[1024,128]{0,1:T(8,128)(2,1)S(1)}, u32[]{:S(2)}, u32[]{:S(2)}) collective-permute-start(bf16[1024,128]{0,1:T(8,128)(2,1)S(1)} %pad_maximum_fusion.31), channel_id=1, source_target_pairs={{0,4},{4,8},{8,12},{12,0},{1,5},{5,9},{9,13},{13,1},{2,6},{6,10},{... | collective-permute-start | bytes 786440 | tf_op jit(solution)/shard_map/ppermute | solution.py:17
  86.4 22.1 %collective-permute-start.36 = (bf16[1024,256]{0,1:T(8,128)(2,1)S(1)}, bf16[1024,256]{0,1:T(8,128)(2,1)S(1)}, u32[]{:S(2)}, u32[]{:S(2)}) collective-permute-start(bf16[1024,256]{0,1:T(8,128)(2,1)S(1)} %pad_maximum_fusion.8), channel_id=1, source_target_pairs={{0,12},{4,0},{8,4},{12,8},{1,13},{5,1},{9,5},{13,9},{2,14},{6,2},{... | collective-permute-start | bytes 1572872 | tf_op jit(solution)/shard_map/ppermute | solution.py:17
  86.5 25.1 %collective-permute-start.35 = (bf16[1024,256]{0,1:T(8,128)(2,1)S(1)}, bf16[1024,256]{0,1:T(8,128)(2,1)S(1)}, u32[]{:S(2)}, u32[]{:S(2)}) collective-permute-start(bf16[1024,256]{0,1:T(8,128)(2,1)S(1)} %pad_maximum_fusion.8), channel_id=1, source_target_pairs={{0,4},{4,8},{8,12},{12,0},{1,5},{5,9},{9,13},{13,1},{2,6},{6,10},{... | collective-permute-start | bytes 1572872 | tf_op jit(solution)/shard_map/ppermute | solution.py:17
  88.1 33.7 %collective-permute-start.67 = (bf16[1024,256]{0,1:T(8,128)(2,1)S(1)}, bf16[1024,256]{0,1:T(8,128)(2,1)S(1)}, u32[]{:S(2)}, u32[]{:S(2)}) collective-permute-start(bf16[1024,256]{0,1:T(8,128)(2,1)S(1)} %pad_maximum_fusion.11), channel_id=1, source_target_pairs={{0,8},{4,12},{8,0},{12,4},{1,9},{5,13},{9,1},{13,5},{2,10},{6,14},... | collective-permute-start | bytes 1572872 | tf_op jit(solution)/shard_map/ppermute | solution.py:17
  88.7 42.3 %collective-permute-start.66 = (bf16[1024,256]{0,1:T(8,128)(2,1)S(1)}, bf16[1024,256]{0,1:T(8,128)(2,1)S(1)}, u32[]{:S(2)}, u32[]{:S(2)}) collective-permute-start(bf16[1024,256]{0,1:T(8,128)(2,1)S(1)} %pad_maximum_fusion.11), channel_id=1, source_target_pairs={{0,12},{4,0},{8,4},{12,8},{1,13},{5,1},{9,5},{13,9},{2,14},{6,2},{... | collective-permute-start | bytes 1572872 | tf_op jit(solution)/shard_map/ppermute | solution.py:17
  99.3 27.5 %collective-permute-start.17 = (bf16[1024,512]{0,1:T(8,128)(2,1)S(1)}, bf16[1024,512]{0,1:T(8,128)(2,1)S(1)}, u32[]{:S(2)}, u32[]{:S(2)}) collective-permute-start(bf16[1024,512]{0,1:T(8,128)(2,1)S(1)} %pad_maximum_fusion), channel_id=1, source_target_pairs={{0,64},{64,0},{1,65},{65,1},{2,66},{66,2},{3,67},{67,3},{4,68},{68... | collective-permute-start | bytes 3145736 | tf_op jit(solution)/shard_map/ppermute | solution.py:36
  108.5 25.3 %collective-permute-start.65 = (bf16[1024,256]{0,1:T(8,128)(2,1)S(1)}, bf16[1024,256]{0,1:T(8,128)(2,1)S(1)}, u32[]{:S(2)}, u32[]{:S(2)}) collective-permute-start(bf16[1024,256]{0,1:T(8,128)(2,1)S(1)} %pad_maximum_fusion.11), channel_id=1, source_target_pairs={{0,4},{4,8},{8,12},{12,0},{1,5},{5,9},{9,13},{13,1},{2,6},{6,10},{... | collective-permute-start | bytes 1572872 | tf_op jit(solution)/shard_map/ppermute | solution.py:17
  111.8 52.0 %collective-permute-start.39 = (bf16[1024,512]{0,1:T(8,128)(2,1)S(1)}, bf16[1024,512]{0,1:T(8,128)(2,1)S(1)}, u32[]{:S(2)}, u32[]{:S(2)}) collective-permute-start(bf16[1024,512]{0,1:T(8,128)(2,1)S(1)} %pad_maximum_fusion.2), channel_id=1, source_target_pairs={{0,64},{64,0},{1,65},{65,1},{2,66},{66,2},{3,67},{67,3},{4,68},{68... | collective-permute-start | bytes 3145736 | tf_op jit(solution)/shard_map/ppermute | solution.py:36
  121.8 32.5 %collective-permute-start.38 = (bf16[1024,512]{0,1:T(8,128)(2,1)S(1)}, bf16[1024,512]{0,1:T(8,128)(2,1)S(1)}, u32[]{:S(2)}, u32[]{:S(2)}) collective-permute-start(bf16[1024,512]{0,1:T(8,128)(2,1)S(1)} %pad_maximum_fusion.1), channel_id=1, source_target_pairs={{0,64},{64,0},{1,65},{65,1},{2,66},{66,2},{3,67},{67,3},{4,68},{68... | collective-permute-start | bytes 3145736 | tf_op jit(solution)/shard_map/ppermute | solution.py:36
  158.8 64.1 %collective-permute-start.71 = (bf16[1024,512]{0,1:T(8,128)(2,1)S(1)}, bf16[1024,512]{0,1:T(8,128)(2,1)S(1)}, u32[]{:S(2)}, u32[]{:S(2)}) collective-permute-start(bf16[1024,512]{0,1:T(8,128)(2,1)S(1)} %pad_maximum_fusion.4), channel_id=1, source_target_pairs={{0,64},{64,0},{1,65},{65,1},{2,66},{66,2},{3,67},{67,3},{4,68},{68... | collective-permute-start | bytes 3145736 | tf_op jit(solution)/shard_map/ppermute | solution.py:36
  161.1 52.5 %collective-permute-start.72 = (bf16[1024,512]{0,1:T(8,128)(2,1)S(1)}, bf16[1024,512]{0,1:T(8,128)(2,1)S(1)}, u32[]{:S(2)}, u32[]{:S(2)}) collective-permute-start(bf16[1024,512]{0,1:T(8,128)(2,1)S(1)} %pad_maximum_fusion.5), channel_id=1, source_target_pairs={{0,64},{64,0},{1,65},{65,1},{2,66},{66,2},{3,67},{67,3},{4,68},{68... | collective-permute-start | bytes 3145736 | tf_op jit(solution)/shard_map/ppermute | solution.py:36
  213.6 142.8 %collective-permute-start.149 = (bf16[256,512]{1,0:T(8,128)(2,1)S(1)}, bf16[256,512]{1,0:T(8,128)(2,1)}, u32[]{:S(2)}, u32[]{:S(2)}) collective-permute-start(bf16[256,512]{1,0:T(8,128)(2,1)S(1)} %get-tuple-element.298), channel_id=1, source_target_pairs={{0,64},{64,0},{1,65},{65,1},{2,66},{66,2},{3,67},{67,3},{4,68},{68... | collective-permute-start | bytes 786440 | tf_op jit(solution)/shard_map/ppermute | solution.py:36
  217.6 45.8 %collective-permute-start.120 = (bf16[256,512]{1,0:T(8,128)(2,1)S(1)}, bf16[256,512]{1,0:T(8,128)(2,1)S(1)}, u32[]{:S(2)}, u32[]{:S(2)}) collective-permute-start(bf16[256,512]{1,0:T(8,128)(2,1)S(1)} %get-tuple-element.31), channel_id=1, source_target_pairs={{0,64},{64,0},{1,65},{65,1},{2,66},{66,2},{3,67},{67,3},{4,68},{68... | collective-permute-start | bytes 786440 | tf_op jit(solution)/shard_map/ppermute | solution.py:36
  229.1 21.6 %collective-permute-start.139 = (bf16[256,512]{1,0:T(8,128)(2,1)S(1)}, bf16[256,512]{1,0:T(8,128)(2,1)S(1)}, u32[]{:S(2)}, u32[]{:S(2)}) collective-permute-start(bf16[256,512]{1,0:T(8,128)(2,1)S(1)} %fusion.11), channel_id=1, source_target_pairs={{0,64},{64,0},{1,65},{65,1},{2,66},{66,2},{3,67},{67,3},{4,68},{68... | collective-permute-start | bytes 786440 | tf_op jit(solution)/shard_map/ppermute | solution.py:36
  250.7 117.2 %collective-permute-start.100 = (bf16[64,1024]{1,0:T(8,128)(2,1)}, bf16[64,1024]{1,0:T(8,128)(2,1)S(1)}, u32[]{:S(2)}, u32[]{:S(2)}) collective-permute-start(bf16[64,1024]{1,0:T(8,128)(2,1)} %get-tuple-element.150), channel_id=1, source_target_pairs={{0,3},{1,0},{2,1},{3,2},{4,7},{5,4},{6,5},{7,6},{8,11},{9,8},{10,9... | collective-permute-start | bytes 393224 | tf_op jit(solution)/shard_map/ppermute | solution.py:17
  284.5 16.7 %collective-permute-start.87 = (bf16[64,1024]{1,0:T(8,128)(2,1)S(1)}, bf16[64,1024]{1,0:T(8,128)(2,1)S(1)}, u32[]{:S(2)}, u32[]{:S(2)}) collective-permute-start(bf16[64,1024]{1,0:T(8,128)(2,1)S(1)} %get-tuple-element.83), channel_id=1, source_target_pairs={{0,2},{1,3},{2,0},{3,1},{4,6},{5,7},{6,4},{7,5},{8,10},{9,11},{10,... | collective-permute-start | bytes 393224 | tf_op jit(solution)/shard_map/ppermute | solution.py:17
  288.6 19.4 %collective-permute-start.86 = (bf16[64,1024]{1,0:T(8,128)(2,1)S(1)}, bf16[64,1024]{1,0:T(8,128)(2,1)S(1)}, u32[]{:S(2)}, u32[]{:S(2)}) collective-permute-start(bf16[64,1024]{1,0:T(8,128)(2,1)S(1)} %get-tuple-element.83), channel_id=1, source_target_pairs={{0,3},{1,0},{2,1},{3,2},{4,7},{5,4},{6,5},{7,6},{8,11},{9,8},{10,9... | collective-permute-start | bytes 393224 | tf_op jit(solution)/shard_map/ppermute | solution.py:17
  326.3 45.1 %collective-permute-start.102 = (bf16[64,1024]{1,0:T(8,128)(2,1)S(1)}, bf16[64,1024]{1,0:T(8,128)(2,1)S(1)}, u32[]{:S(2)}, u32[]{:S(2)}) collective-permute-start(bf16[64,1024]{1,0:T(8,128)(2,1)S(1)} %get-tuple-element.151), channel_id=1, source_target_pairs={{0,2},{1,3},{2,0},{3,1},{4,6},{5,7},{6,4},{7,5},{8,10},{9,11},{10,... | collective-permute-start | bytes 393224 | tf_op jit(solution)/shard_map/ppermute | solution.py:17
  342.7 30.4 %collective-permute-start.101 = (bf16[64,1024]{1,0:T(8,128)(2,1)S(1)}, bf16[64,1024]{1,0:T(8,128)(2,1)S(1)}, u32[]{:S(2)}, u32[]{:S(2)}) collective-permute-start(bf16[64,1024]{1,0:T(8,128)(2,1)S(1)} %get-tuple-element.152), channel_id=1, source_target_pairs={{0,1},{1,2},{2,3},{3,0},{4,5},{5,6},{6,7},{7,4},{8,9},{9,10},{10,1... | collective-permute-start | bytes 393224 | tf_op jit(solution)/shard_map/ppermute | solution.py:17
  373.1 34.7 %collective-permute-start.150 = (bf16[1024,256]{0,1:T(8,128)(2,1)}, bf16[1024,256]{0,1:T(8,128)(2,1)}, u32[]{:S(2)}, u32[]{:S(2)}) collective-permute-start(bf16[1024,256]{0,1:T(8,128)(2,1)} %pad_maximum_fusion.20), channel_id=1, source_target_pairs={{0,12},{4,0},{8,4},{12,8},{1,13},{5,1},{9,5},{13,9},{2,14},{6,2},{... | collective-permute-start | bytes 1572872 | tf_op jit(solution)/shard_map/ppermute | solution.py:17
  373.9 40.0 %collective-permute-start.151 = (bf16[1024,256]{0,1:T(8,128)(2,1)}, bf16[1024,256]{0,1:T(8,128)(2,1)}, u32[]{:S(2)}, u32[]{:S(2)}) collective-permute-start(bf16[1024,256]{0,1:T(8,128)(2,1)} %pad_maximum_fusion.21), channel_id=1, source_target_pairs={{0,4},{4,8},{8,12},{12,0},{1,5},{5,9},{9,13},{13,1},{2,6},{6,10},{... | collective-permute-start | bytes 1572872 | tf_op jit(solution)/shard_map/ppermute | solution.py:17
  395.7 18.3 %collective-permute-start.152 = (bf16[1024,256]{0,1:T(8,128)(2,1)S(1)}, bf16[1024,256]{0,1:T(8,128)(2,1)S(1)}, u32[]{:S(2)}, u32[]{:S(2)}) collective-permute-start(bf16[1024,256]{0,1:T(8,128)(2,1)S(1)} %copy-done.11), channel_id=1, source_target_pairs={{0,8},{4,12},{8,0},{12,4},{1,9},{5,13},{9,1},{13,5},{2,10},{6,14},... | collective-permute-start | bytes 1572872 | tf_op jit(solution)/shard_map/ppermute | solution.py:17
  403.3 45.2 %collective-permute-start.162 = (bf16[256,256]{0,1:T(8,128)(2,1)S(1)}, bf16[256,256]{0,1:T(8,128)(2,1)S(1)}, u32[]{:S(2)}, u32[]{:S(2)}) collective-permute-start(bf16[256,256]{0,1:T(8,128)(2,1)S(1)} %copy-done.26), channel_id=1, source_target_pairs={{0,48},{16,0},{32,16},{48,32},{1,49},{17,1},{33,17},{49,33},{2,50}... | collective-permute-start | bytes 393224 | tf_op jit(solution)/shard_map/ppermute | solution.py:17
  406.0 43.7 %collective-permute-start.164 = (bf16[256,256]{0,1:T(8,128)(2,1)S(1)}, bf16[256,256]{0,1:T(8,128)(2,1)S(1)}, u32[]{:S(2)}, u32[]{:S(2)}) collective-permute-start(bf16[256,256]{0,1:T(8,128)(2,1)S(1)} %copy-done.25), channel_id=1, source_target_pairs={{0,32},{16,48},{32,0},{48,16},{1,33},{17,49},{33,1},{49,17},{2,34}... | collective-permute-start | bytes 393224 | tf_op jit(solution)/shard_map/ppermute | solution.py:17
  427.4 24.0 %collective-permute-start.163 = (bf16[256,256]{0,1:T(8,128)(2,1)S(1)}, bf16[256,256]{0,1:T(8,128)(2,1)S(1)}, u32[]{:S(2)}, u32[]{:S(2)}) collective-permute-start(bf16[256,256]{0,1:T(8,128)(2,1)S(1)} %copy-done.24), channel_id=1, source_target_pairs={{0,16},{16,32},{32,48},{48,0},{1,17},{17,33},{33,49},{49,1},{2,18}... | collective-permute-start | bytes 393224 | tf_op jit(solution)/shard_map/ppermute | solution.py:17
  428.9 23.6 %collective-permute-start.153 = (bf16[256,256]{0,1:T(8,128)(2,1)S(1)}, bf16[256,256]{0,1:T(8,128)(2,1)S(1)}, u32[]{:S(2)}, u32[]{:S(2)}) collective-permute-start(bf16[256,256]{0,1:T(8,128)(2,1)S(1)} %get-tuple-element.144), channel_id=1, source_target_pairs={{0,48},{16,0},{32,16},{48,32},{1,49},{17,1},{33,17},{49,33},{2,50}... | collective-permute-start | bytes 393224 | tf_op jit(solution)/shard_map/ppermute | solution.py:17
  449.8 22.0 %collective-permute-start.124 = (bf16[256,128]{0,1:T(8,128)(2,1)S(1)}, bf16[256,128]{0,1:T(8,128)(2,1)S(1)}, u32[]{:S(2)}, u32[]{:S(2)}) collective-permute-start(bf16[256,128]{0,1:T(8,128)(2,1)S(1)} %copy-done.29), channel_id=1, source_target_pairs={{0,48},{16,0},{32,16},{48,32},{1,49},{17,1},{33,17},{49,33},{2,50}... | collective-permute-start | bytes 196616 | tf_op jit(solution)/shard_map/ppermute | solution.py:17
  451.3 21.9 %collective-permute-start.126 = (bf16[256,128]{0,1:T(8,128)(2,1)S(1)}, bf16[256,128]{0,1:T(8,128)(2,1)S(1)}, u32[]{:S(2)}, u32[]{:S(2)}) collective-permute-start(bf16[256,128]{0,1:T(8,128)(2,1)S(1)} %copy-done.28), channel_id=1, source_target_pairs={{0,32},{16,48},{32,0},{48,16},{1,33},{17,49},{33,1},{49,17},{2,34}... | collective-permute-start | bytes 196616 | tf_op jit(solution)/shard_map/ppermute | solution.py:17
  (186 other events, 1944.6 us)
